TPU v7x, 32 devices: a whole 2x2x4 slice. The times are simulated.
32 devices in a mesh: dp: 8 (over z, x), seq: 4 (over y, core).
Axes of the slice: x: 2, y: 2, z: 4, core: 2. Of those that a mesh axis runs over, the one named last changes fastest.
Arguments:
- block_input: bfloat16 [8, 1024, 1024], P('dp', 'seq'), may hold values from -6 to 6
- output_grad: bfloat16 [8, 1024, 1024], P('dp', 'seq'), may hold values from -9 to 9
- row_lengths: int32 [8], P('dp'), may hold values from 341 to 1024, as said below
- qkv_weight: float32 [2, 1024, 3, 1024], P(None, 'dp', None, 'seq'), may hold values from -0.1875 to 0.1875
- proj_weight: float32 [2, 1024, 1024], P(None, 'seq', 'dp'), may hold values from -0.5 to 0.5
- up_weight: float32 [2, 1024, 4096], P(None, 'dp', 'seq'), may hold values from -0.1875 to 0.1875
- down_weight: float32 [2, 4096, 1024], P(None, 'seq', 'dp'), may hold values from -0.125 to 0.125
- norm_params: float32 [2, 4, 1024], P(None, None, ('dp', 'seq')), may hold values from -2 to 2
- qkv_first: float32 [2, 1024, 3, 1024], P(None, 'dp', None, 'seq'), may hold values from -0.00012207031 to 0.00012207031
- proj_first: float32 [2, 1024, 1024], P(None, 'seq', 'dp'), may hold values from -0.00012207031 to 0.00012207031
- up_first: float32 [2, 1024, 4096], P(None, 'dp', 'seq'), may hold values from -0.00012207031 to 0.00012207031
- down_first: float32 [2, 4096, 1024], P(None, 'seq', 'dp'), may hold values from -0.00012207031 to 0.00012207031
- norm_first: float32 [2, 4, 1024], P(None, None, ('dp', 'seq')), may hold values from -0.00012207031 to 0.00012207031
- qkv_second: float32 [2, 1024, 3, 1024], P(None, 'dp', None, 'seq'), may hold values from 1.3113022e-10 to 5.1657356e-10
- proj_second: float32 [2, 1024, 1024], P(None, 'seq', 'dp'), may hold values from 1.3113022e-10 to 5.1657356e-10
- up_second: float32 [2, 1024, 4096], P(None, 'dp', 'seq'), may hold values from 1.3113022e-10 to 5.1657356e-10
- down_second: float32 [2, 4096, 1024], P(None, 'seq', 'dp'), may hold values from 1.3113022e-10 to 5.1657356e-10
- norm_second: float32 [2, 4, 1024], P(None, None, ('dp', 'seq')), may hold values from 1.3113022e-10 to 5.1657356e-10
Outputs:
- block_output: float32 [8, 1024, 1024], P('dp', 'seq')
- input_grad: float32 [8, 1024, 1024], P('dp', 'seq')
- grad_norm: float32 [], replicated
- qkv_grad: float32 [2, 1024, 3, 1024], P(None, 'dp', None, 'seq')
- proj_grad: float32 [2, 1024, 1024], P(None, 'seq', 'dp')
- up_grad: float32 [2, 1024, 4096], P(None, 'dp', 'seq')
- down_grad: float32 [2, 4096, 1024], P(None, 'seq', 'dp')
- norm_grad: float32 [2, 4, 1024], P(None, None, ('dp', 'seq'))
- qkv_momentum: float32 [2, 1024, 3, 1024], P(None, 'dp', None, 'seq')
- proj_momentum: float32 [2, 1024, 1024], P(None, 'seq', 'dp')
- up_momentum: float32 [2, 1024, 4096], P(None, 'dp', 'seq')
- down_momentum: float32 [2, 4096, 1024], P(None, 'seq', 'dp')
- norm_momentum: float32 [2, 4, 1024], P(None, None, ('dp', 'seq'))
- qkv_variance: float32 [2, 1024, 3, 1024], P(None, 'dp', None, 'seq')
- proj_variance: float32 [2, 1024, 1024], P(None, 'seq', 'dp')
- up_variance: float32 [2, 1024, 4096], P(None, 'dp', 'seq')
- down_variance: float32 [2, 4096, 1024], P(None, 'seq', 'dp')
- norm_variance: float32 [2, 4, 1024], P(None, None, ('dp', 'seq'))
- qkv_new: float32 [2, 1024, 3, 1024], P(None, 'dp', None, 'seq')
- proj_new: float32 [2, 1024, 1024], P(None, 'seq', 'dp')
- up_new: float32 [2, 1024, 4096], P(None, 'dp', 'seq')
- down_new: float32 [2, 4096, 1024], P(None, 'seq', 'dp')
- norm_new: float32 [2, 4, 1024], P(None, None, ('dp', 'seq'))
- qkv_copy: bfloat16 [2, 1024, 3, 1024], P(None, 'dp', None, 'seq')
- proj_copy: bfloat16 [2, 1024, 1024], P(None, 'seq', 'dp')
- up_copy: bfloat16 [2, 1024, 4096], P(None, 'dp', 'seq')
- down_copy: bfloat16 [2, 4096, 1024], P(None, 'seq', 'dp')
- norm_copy: bfloat16 [2, 4, 1024], P(None, None, ('dp', 'seq'))
Inputs may be any that keep to these rules, and one draw needn't show every extreme that they name: Slots of row r below row_lengths[r] hold real tokens, the others padding. In every draw one row is 1024 long and one row is 341 long.
All inputs are finite; a program needn't handle non-finite values.
Results may differ from a plain program's by a relative error of at most 0.025.
Values may be sent and summed in bfloat16 or wider, within the bound.
A program may use at most 320 MiB of HBM per device.

v0:
```python
import jax
import jax.numpy as jnp
import numpy as np
from jax import lax
from jax.sharding import PartitionSpec as P

H = 8
HD = 128
STEP = 5


EPS_NORM = 1e-05
BETA_ONE = 0.5
BETA_TWO = 0.75
LEARN_RATE = 0.03
NORM_RATE = 0.3
WEIGHT_DECAY = 0.1
CLIP_NORM = 0.1
ADAM_EPS = 1e-08


def slope_table(head_count):
    return np.power(2.0, -8.0 * (np.arange(head_count) + 1.0) / head_count)


def smooth_act(values):
    return jax.nn.gelu(values, approximate=True)


def smooth_back(upper, grad_act):
    unused, pullback = jax.vjp(smooth_act, upper)
    return pullback(grad_act)[0]


def layer_norm(hidden, gain, bias):
    centre = jnp.mean(hidden, axis=-1, keepdims=True)
    centered = hidden - centre
    variance = jnp.mean(centered * centered, axis=-1, keepdims=True)
    scaled = centered * lax.rsqrt(variance + EPS_NORM)
    return (scaled, scaled * gain + bias)


def norm_back(hidden, gain, grad_out):
    centered = hidden - jnp.mean(hidden, axis=-1, keepdims=True)
    inverse = lax.rsqrt(jnp.mean(centered * centered, axis=-1, keepdims=True) + EPS_NORM)
    scaled = centered * inverse
    grad_scaled = grad_out * gain
    grad_hidden = inverse * (
        grad_scaled
        - jnp.mean(grad_scaled, axis=-1, keepdims=True)
        - scaled * jnp.mean(grad_scaled * scaled, axis=-1, keepdims=True)
    )
    return (grad_hidden, jnp.sum(grad_out * scaled, axis=0), jnp.sum(grad_out, axis=0))


def gather_groups(masters, layer_index):
    qkv_part = masters[0][layer_index].astype(jnp.bfloat16)
    proj_part = masters[1][layer_index].astype(jnp.bfloat16)
    up_part = masters[2][layer_index].astype(jnp.bfloat16)
    down_part = masters[3][layer_index].astype(jnp.bfloat16)
    norm_local = masters[4][layer_index].astype(jnp.bfloat16)
    norm_part = norm_local.reshape(4, 1, norm_local.shape[1])
    return (
        lax.all_gather(qkv_part, "dp", axis=0, tiled=True),
        lax.all_gather(proj_part, "dp", axis=1, tiled=True),
        lax.all_gather(up_part, "dp", axis=0, tiled=True),
        lax.all_gather(down_part, "dp", axis=1, tiled=True),
        lax.all_gather(norm_part, "dp", axis=1, tiled=True),
    )


def order_norm(norm_every):
    return jnp.transpose(norm_every, (1, 2, 0, 3)).reshape(4, -1).astype(jnp.float32)


def reduce_grads(qkv_part, proj_part, up_part, down_part, norm_part):
    group_count = lax.axis_size("dp")
    seq_count = lax.axis_size("seq")
    piece = norm_part.shape[1] // (group_count * seq_count)
    arranged = jnp.transpose(norm_part.reshape(4, group_count, seq_count, piece), (2, 0, 1, 3))
    group_qkv, group_proj, group_up, group_down, group_norm = (
        lax.psum_scatter(
            qkv_part.astype(jnp.bfloat16), "dp", scatter_dimension=0, tiled=True
        ).astype(jnp.float32),
        lax.psum_scatter(
            proj_part.astype(jnp.bfloat16), "dp", scatter_dimension=1, tiled=True
        ).astype(jnp.float32),
        lax.psum_scatter(
            up_part.astype(jnp.bfloat16), "dp", scatter_dimension=0, tiled=True
        ).astype(jnp.float32),
        lax.psum_scatter(
            down_part.astype(jnp.bfloat16), "dp", scatter_dimension=1, tiled=True
        ).astype(jnp.float32),
        lax.psum_scatter(
            arranged.astype(jnp.bfloat16), "dp", scatter_dimension=2, tiled=True
        ).astype(jnp.float32),
    )
    final_qkv, final_proj, final_up, final_down, final_norm = (
        lax.psum_scatter(
            group_qkv.astype(jnp.bfloat16), "seq", scatter_dimension=2, tiled=True
        ).astype(jnp.float32),
        lax.psum_scatter(
            group_proj.astype(jnp.bfloat16), "seq", scatter_dimension=0, tiled=True
        ).astype(jnp.float32),
        lax.psum_scatter(
            group_up.astype(jnp.bfloat16), "seq", scatter_dimension=1, tiled=True
        ).astype(jnp.float32),
        lax.psum_scatter(
            group_down.astype(jnp.bfloat16), "seq", scatter_dimension=0, tiled=True
        ).astype(jnp.float32),
        lax.psum_scatter(
            group_norm.astype(jnp.bfloat16), "seq", scatter_dimension=0, tiled=True
        ).astype(jnp.float32),
    )
    return (final_qkv, final_proj, final_up, final_down, final_norm.reshape(4, piece))


def block_scores(query_block, key_rows, first_row, slopes, lengths):
    block_rows = query_block.shape[1]
    slot_count = key_rows.shape[1]
    raw = jnp.einsum(
        "rqhd,rkhd->rhqk", query_block, key_rows, preferred_element_type=jnp.float32
    ) * HD ** (-0.5)
    query_pos = first_row + jnp.arange(block_rows, dtype=jnp.int32)
    key_pos = jnp.arange(slot_count, dtype=jnp.int32)
    distance = (key_pos[None, :] - query_pos[:, None]).astype(jnp.float32)
    raw = raw + slopes[None, :, None, None] * distance[None, None]
    causal = key_pos[None, :] <= query_pos[:, None]
    filled = key_pos[None, :] < lengths[:, None]
    allowed = causal[None, None] & filled[:, None, None, :]
    return jnp.where(allowed, raw, -jnp.inf)


def attend_forward(queries, key_rows, values, slopes, lengths):
    row_count, slot_count, head_local, head_size = queries.shape
    block_rows = min(512, slot_count)

    def one_block(block_index, carry):
        context, log_total = carry
        first_row = block_index * block_rows
        query_block = lax.dynamic_slice_in_dim(queries, first_row, block_rows, 1)
        scores = block_scores(query_block, key_rows, first_row, slopes, lengths)
        block_total = jax.nn.logsumexp(scores, axis=3, keepdims=True)
        attention = jnp.exp(scores - block_total).astype(jnp.bfloat16)
        block_context = jnp.einsum(
            "rhqk,rkhd->rqhd", attention, values, preferred_element_type=jnp.float32
        ).astype(jnp.bfloat16)
        context = lax.dynamic_update_slice_in_dim(context, block_context, first_row, 1)
        log_total = lax.dynamic_update_slice_in_dim(log_total, block_total[..., 0], first_row, 2)
        return (context, log_total)

    initial = (
        jnp.zeros(queries.shape, jnp.bfloat16),
        jnp.zeros((row_count, head_local, slot_count), jnp.float32),
    )
    return lax.fori_loop(0, slot_count // block_rows, one_block, initial)


def attend_backward(queries, key_rows, values, grad_context, log_total, slopes, lengths):
    row_count, slot_count, head_local, head_size = queries.shape
    block_rows = min(512, slot_count)
    score_scale = HD ** (-0.5)

    def one_block(block_index, carry):
        grad_queries, grad_keys, grad_values = carry
        first_row = block_index * block_rows
        query_block = lax.dynamic_slice_in_dim(queries, first_row, block_rows, 1)
        grad_block = lax.dynamic_slice_in_dim(grad_context, first_row, block_rows, 1)
        scores = block_scores(query_block, key_rows, first_row, slopes, lengths)
        block_total = lax.dynamic_slice_in_dim(log_total, first_row, block_rows, 2)
        attention = jnp.exp(scores - block_total[..., None])
        grad_attention = jnp.einsum(
            "rqhd,rkhd->rhqk", grad_block, values, preferred_element_type=jnp.float32
        )
        inner_sum = jnp.sum(attention * grad_attention, axis=3, keepdims=True)
        grad_scores = (attention * (grad_attention - inner_sum)).astype(jnp.bfloat16)
        block_grad = (
            jnp.einsum("rhqk,rkhd->rqhd", grad_scores, key_rows, preferred_element_type=jnp.float32)
            * score_scale
        ).astype(jnp.bfloat16)
        grad_queries = lax.dynamic_update_slice_in_dim(grad_queries, block_grad, first_row, 1)
        grad_keys = (
            grad_keys
            + jnp.einsum(
                "rhqk,rqhd->rkhd", grad_scores, query_block, preferred_element_type=jnp.float32
            )
            * score_scale
        )
        grad_values = grad_values + jnp.einsum(
            "rhqk,rqhd->rkhd",
            attention.astype(jnp.bfloat16),
            grad_block,
            preferred_element_type=jnp.float32,
        )
        return (grad_queries, grad_keys, grad_values)

    initial = (
        jnp.zeros(queries.shape, jnp.bfloat16),
        jnp.zeros(queries.shape, jnp.float32),
        jnp.zeros(queries.shape, jnp.float32),
    )
    return lax.fori_loop(0, slot_count // block_rows, one_block, initial)


def adam_update(master, grad, first, second, factor, fix_one, fix_two, decay, rate):
    clipped = grad * factor
    momentum = BETA_ONE * first + (1.0 - BETA_ONE) * clipped
    variance = BETA_TWO * second + (1.0 - BETA_TWO) * clipped * clipped
    step_size = momentum / fix_one / (jnp.sqrt(variance / fix_two) + ADAM_EPS) + decay * master
    fresh = master - rate * step_size
    return (momentum, variance, fresh, fresh.astype(jnp.bfloat16))


def body(
    block_input,
    output_grad,
    row_lengths,
    qkv_weight,
    proj_weight,
    up_weight,
    down_weight,
    norm_params,
    qkv_first,
    proj_first,
    up_first,
    down_first,
    norm_first,
    qkv_second,
    proj_second,
    up_second,
    down_second,
    norm_second,
):
    masters = (qkv_weight, proj_weight, up_weight, down_weight, norm_params)
    row_count, local_slots, model_width = block_input.shape
    seq_count = lax.axis_size("seq")
    head_local = H // seq_count
    token_count = row_count * local_slots
    layer_count = qkv_weight.shape[0]
    table = jnp.asarray(slope_table(H), jnp.float32)
    head_ids = lax.axis_index("seq") * head_local + jnp.arange(head_local, dtype=jnp.int32)
    slopes = jnp.sum(
        jnp.where(
            jnp.arange(H, dtype=jnp.int32)[None, :] == head_ids[:, None], table[None, :], 0.0
        ),
        axis=1,
    )
    hidden = block_input.astype(jnp.float32).reshape(token_count, model_width)
    saved = []
    for layer_index in range(layer_count):
        qkv_group, proj_group, up_group, down_group, norm_group = gather_groups(
            masters, layer_index
        )
        qkv_all, w_proj, w_up, w_down, norm_every = (
            lax.all_gather(qkv_group, "seq", axis=2, tiled=True),
            lax.all_gather(proj_group, "seq", axis=0, tiled=True),
            lax.all_gather(up_group, "seq", axis=1, tiled=True),
            lax.all_gather(down_group, "seq", axis=0, tiled=True),
            lax.all_gather(norm_group[None], "seq", axis=0, tiled=True),
        )
        w_qkv = qkv_all.reshape(model_width, -1)
        norm_rows = order_norm(norm_every)
        unused, normed = layer_norm(hidden, norm_rows[0], norm_rows[1])
        normed_low = normed.astype(jnp.bfloat16)
        projected = jnp.dot(normed_low, w_qkv, preferred_element_type=jnp.float32).astype(
            jnp.bfloat16
        )
        projected = projected.reshape(row_count, local_slots, 3, H, HD)
        spread = lax.all_to_all(projected, "seq", split_axis=3, concat_axis=1, tiled=True)
        context, log_total = attend_forward(
            spread[:, :, 0], spread[:, :, 1], spread[:, :, 2], slopes, row_lengths
        )
        context_tokens = lax.all_to_all(
            context, "seq", split_axis=1, concat_axis=2, tiled=True
        ).reshape(token_count, model_width)
        middle = hidden + jnp.dot(context_tokens, w_proj, preferred_element_type=jnp.float32)
        unused, normed_two = layer_norm(middle, norm_rows[2], norm_rows[3])
        upper = jnp.dot(normed_two.astype(jnp.bfloat16), w_up, preferred_element_type=jnp.float32)
        act_low = smooth_act(upper).astype(jnp.bfloat16)
        following = middle + jnp.dot(act_low, w_down, preferred_element_type=jnp.float32)
        saved.append(
            (
                hidden,
                middle,
                spread,
                log_total,
                context_tokens,
                act_low,
                upper,
                normed_low,
                None,
                (w_qkv, w_proj, w_up, w_down, norm_rows),
            )
        )
        hidden = following
    block_output = hidden.reshape(row_count, local_slots, model_width)
    positions = lax.axis_index("seq") * local_slots + jnp.arange(local_slots, dtype=jnp.int32)
    token_mask = (positions[None, :] < row_lengths[:, None]).astype(jnp.float32)
    grad_hidden = (output_grad.astype(jnp.float32) * token_mask[:, :, None]).reshape(
        token_count, model_width
    )
    reduced_all = [None] * layer_count
    for layer_index in reversed(range(layer_count)):
        (
            hidden_in,
            middle,
            spread,
            log_total,
            context_saved,
            act_low,
            upper,
            normed_kept,
            normed_two_kept,
            weights,
        ) = saved[layer_index]
        w_qkv, w_proj, w_up, w_down, norm_rows = weights
        grad_ffn = grad_hidden.astype(jnp.bfloat16)
        unused, normed_two = layer_norm(middle, norm_rows[2], norm_rows[3])
        down_grad = jnp.einsum("tf,td->fd", act_low, grad_ffn, preferred_element_type=jnp.float32)
        grad_act = jnp.einsum("td,fd->tf", grad_ffn, w_down, preferred_element_type=jnp.float32)
        grad_upper = smooth_back(upper, grad_act).astype(jnp.bfloat16)
        up_grad = jnp.einsum(
            "td,tf->df",
            normed_two.astype(jnp.bfloat16),
            grad_upper,
            preferred_element_type=jnp.float32,
        )
        grad_normed_two = jnp.einsum(
            "tf,df->td", grad_upper, w_up, preferred_element_type=jnp.float32
        )
        grad_middle_norm, gain_two, bias_two = norm_back(middle, norm_rows[2], grad_normed_two)
        grad_middle = grad_hidden + grad_middle_norm
        grad_branch = grad_middle.astype(jnp.bfloat16)
        proj_grad = jnp.einsum(
            "td,te->de", context_saved, grad_branch, preferred_element_type=jnp.float32
        )
        grad_context = jnp.einsum(
            "te,de->td", grad_branch, w_proj, preferred_element_type=jnp.float32
        ).astype(jnp.bfloat16)
        grad_context = lax.all_to_all(
            grad_context.reshape(row_count, local_slots, H, HD),
            "seq",
            split_axis=2,
            concat_axis=1,
            tiled=True,
        )
        grad_queries, grad_keys, grad_values = attend_backward(
            spread[:, :, 0],
            spread[:, :, 1],
            spread[:, :, 2],
            grad_context,
            log_total,
            slopes,
            row_lengths,
        )
        grad_spread = jnp.stack(
            (grad_queries, grad_keys.astype(jnp.bfloat16), grad_values.astype(jnp.bfloat16)), axis=2
        )
        grad_projected = lax.all_to_all(
            grad_spread, "seq", split_axis=1, concat_axis=3, tiled=True
        ).reshape(token_count, 3 * model_width)
        qkv_grad = jnp.einsum(
            "td,te->de", normed_kept, grad_projected, preferred_element_type=jnp.float32
        )
        qkv_grad = qkv_grad.reshape(model_width, 3, model_width)
        grad_normed = jnp.einsum(
            "te,de->td", grad_projected, w_qkv, preferred_element_type=jnp.float32
        )
        grad_input_norm, gain_one, bias_one = norm_back(hidden_in, norm_rows[0], grad_normed)
        grad_hidden = grad_middle + grad_input_norm
        norm_grad = jnp.stack((gain_one, bias_one, gain_two, bias_two), axis=0)
        reduced_all[layer_index] = reduce_grads(qkv_grad, proj_grad, up_grad, down_grad, norm_grad)
    input_grad = grad_hidden.reshape(row_count, local_slots, model_width)
    stacked = [
        jnp.stack([layer_grads[position] for layer_grads in reduced_all], axis=0)
        for position in range(5)
    ]
    square_sum = (
        jnp.sum(stacked[0] * stacked[0])
        + jnp.sum(stacked[1] * stacked[1])
        + jnp.sum(stacked[2] * stacked[2])
        + jnp.sum(stacked[3] * stacked[3])
        + jnp.sum(stacked[4] * stacked[4])
    )
    grad_norm = jnp.sqrt(lax.psum(square_sum, ("dp", "seq")))
    factor = CLIP_NORM / jnp.maximum(grad_norm, CLIP_NORM)
    fix_one = 1.0 - BETA_ONE**STEP
    fix_two = 1.0 - BETA_TWO**STEP
    qkv_out = adam_update(
        qkv_weight,
        stacked[0],
        qkv_first,
        qkv_second,
        factor,
        fix_one,
        fix_two,
        WEIGHT_DECAY,
        LEARN_RATE,
    )
    proj_out = adam_update(
        proj_weight,
        stacked[1],
        proj_first,
        proj_second,
        factor,
        fix_one,
        fix_two,
        WEIGHT_DECAY,
        LEARN_RATE,
    )
    up_out = adam_update(
        up_weight,
        stacked[2],
        up_first,
        up_second,
        factor,
        fix_one,
        fix_two,
        WEIGHT_DECAY,
        LEARN_RATE,
    )
    down_out = adam_update(
        down_weight,
        stacked[3],
        down_first,
        down_second,
        factor,
        fix_one,
        fix_two,
        WEIGHT_DECAY,
        LEARN_RATE,
    )
    norm_out = adam_update(
        norm_params, stacked[4], norm_first, norm_second, factor, fix_one, fix_two, 0.0, NORM_RATE
    )
    return (
        block_output,
        input_grad,
        grad_norm,
        stacked[0],
        stacked[1],
        stacked[2],
        stacked[3],
        stacked[4],
        qkv_out[0],
        proj_out[0],
        up_out[0],
        down_out[0],
        norm_out[0],
        qkv_out[1],
        proj_out[1],
        up_out[1],
        down_out[1],
        norm_out[1],
        qkv_out[2],
        proj_out[2],
        up_out[2],
        down_out[2],
        norm_out[2],
        qkv_out[3],
        proj_out[3],
        up_out[3],
        down_out[3],
        norm_out[3],
    )


def solution(mesh):
    return jax.shard_map(
        body,
        mesh=mesh,
        in_specs=(
            P("dp", "seq", None),
            P("dp", "seq", None),
            P("dp"),
            P(None, "dp", None, "seq"),
            P(None, "seq", "dp"),
            P(None, "dp", "seq"),
            P(None, "seq", "dp"),
            P(None, None, ("dp", "seq")),
            P(None, "dp", None, "seq"),
            P(None, "seq", "dp"),
            P(None, "dp", "seq"),
            P(None, "seq", "dp"),
            P(None, None, ("dp", "seq")),
            P(None, "dp", None, "seq"),
            P(None, "seq", "dp"),
            P(None, "dp", "seq"),
            P(None, "seq", "dp"),
            P(None, None, ("dp", "seq")),
        ),
        out_specs=(
            P("dp", "seq", None),
            P("dp", "seq", None),
            P(),
            P(None, "dp", None, "seq"),
            P(None, "seq", "dp"),
            P(None, "dp", "seq"),
            P(None, "seq", "dp"),
            P(None, None, ("dp", "seq")),
            P(None, "dp", None, "seq"),
            P(None, "seq", "dp"),
            P(None, "dp", "seq"),
            P(None, "seq", "dp"),
            P(None, None, ("dp", "seq")),
            P(None, "dp", None, "seq"),
            P(None, "seq", "dp"),
            P(None, "dp", "seq"),
            P(None, "seq", "dp"),
            P(None, None, ("dp", "seq")),
            P(None, "dp", None, "seq"),
            P(None, "seq", "dp"),
            P(None, "dp", "seq"),
            P(None, "seq", "dp"),
            P(None, None, ("dp", "seq")),
            P(None, "dp", None, "seq"),
            P(None, "seq", "dp"),
            P(None, "dp", "seq"),
            P(None, "seq", "dp"),
            P(None, None, ("dp", "seq")),
        ),
        check_vma=False,
    )
```

profile of v0, /device:TPU:0, one launch (start us, length us, event | category | flops | bytes accessed | tf_op | source)
XLA Modules:
  0.0 2055.9 jit_solution(10656748940835077363)
XLA Ops:
  13.9 44.8 %all-gather.35.cloned.1.call-done = bf16[1,1024,3,256]{1,3,2,0:T(8,128)(2,1)} async-done(((bf16[1,128,3,256]{1,3,2,0:T(8,128)(2,1)}), bf16[1,1024,3,256]{1,3,2,0:T(8,128)(2,1)}) %all-gather.35.cloned.1.call-update) | async-done | bytes 1572880 | tf_op jit(solution)/shard_map/all_gather | solution.py:64
  59.6 30.3 %all-gather.4 = bf16[1,256,1024]{2,1,0:T(8,128)(2,1)} all-gather(bf16[1,256,128]{2,1,0:T(8,128)(2,1)S(1)} %get-tuple-element.908), channel_id=6, replica_groups=mesh['dp'=8,'seq'=4] {'dp'}, dimensions={2}, use_global_device_ids=true | all-gather | bytes 589824 | tf_op jit(solution)/shard_map/all_gather | solution.py:65
  112.8 52.1 %all-gather.45.cloned.1.call-done = bf16[1,1024,1024]{2,1,0:T(8,128)(2,1)} async-done(((bf16[1,1024,128]{2,1,0:T(8,128)(2,1)}), bf16[1,1024,1024]{2,1,0:T(8,128)(2,1)}) %all-gather.45.cloned.1.call-update) | async-done | bytes 2097168 | tf_op jit(solution)/shard_map/all_gather | solution.py:67
  165.0 45.9 %all-gather.49.cloned.1.call-done = bf16[1,1024,3,256]{1,3,2,0:T(8,128)(2,1)} async-done(((bf16[1,128,3,256]{1,3,2,0:T(8,128)(2,1)}), bf16[1,1024,3,256]{1,3,2,0:T(8,128)(2,1)}) %all-gather.49.cloned.1.call-update) | async-done | bytes 1572880 | tf_op jit(solution)/shard_map/all_gather | solution.py:64
  211.0 30.2 %all-gather.14 = bf16[1,256,1024]{2,1,0:T(8,128)(2,1)} all-gather(bf16[1,256,128]{2,1,0:T(8,128)(2,1)S(1)} %get-tuple-element.907), channel_id=16, replica_groups=mesh['dp'=8,'seq'=4] {'dp'}, dimensions={2}, use_global_device_ids=true | all-gather | bytes 589824 | tf_op jit(solution)/shard_map/all_gather | solution.py:65
  264.5 30.5 %all-gather = bf16[1,4,256]{1,0,2:T(2,128)(2,1)S(1)} all-gather(bf16[1,4,32]{1,0,2:T(2,128)(2,1)S(1)} %get-tuple-element.918), channel_id=2, replica_groups=mesh['dp'=8,'seq'=4] {'dp'}, dimensions={2}, use_global_device_ids=true | all-gather | bytes 2304 | tf_op jit(solution)/shard_map/all_gather | solution.py:68
  321.2 31.0 %all-gather.10 = bf16[1,4,256]{1,0,2:T(2,128)(2,1)S(1)} all-gather(bf16[1,4,32]{1,0,2:T(2,128)(2,1)S(1)} %get-tuple-element.917), channel_id=12, replica_groups=mesh['dp'=8,'seq'=4] {'dp'}, dimensions={2}, use_global_device_ids=true | all-gather | bytes 2304 | tf_op jit(solution)/shard_map/all_gather | solution.py:68
  396.3 57.0 %all-gather.43.cloned.1.call-done = bf16[1,1024,4096]{2,1,0:T(8,128)(2,1)} async-done(((bf16[1,1024,1024]{2,1,0:T(8,128)(2,1)}), bf16[1,1024,4096]{2,1,0:T(8,128)(2,1)}) %all-gather.43.cloned.1.call-update) | async-done | bytes 8388624 | tf_op jit(solution)/shard_map/all_gather | solution.py:257
  461.1 51.9 %all-gather.47.cloned.1.call-done = bf16[1,4096,1024]{2,1,0:T(8,128)(2,1)} async-done(((bf16[1,1024,1024]{2,1,0:T(8,128)(2,1)}), bf16[1,4096,1024]{2,1,0:T(8,128)(2,1)}) %all-gather.47.cloned.1.call-update) | async-done | bytes 8388624 | tf_op jit(solution)/shard_map/all_gather | solution.py:258
  520.7 40.2 %all-gather.51.cloned.1.call-done = bf16[1,1024,3,1024]{1,3,2,0:T(8,128)(2,1)} async-done(((bf16[1,1024,3,256]{1,3,2,0:T(8,128)(2,1)}), bf16[1,1024,3,1024]{1,3,2,0:T(8,128)(2,1)}) %all-gather.51.cloned.1.call-update) | async-done | bytes 6291472 | tf_op jit(solution)/shard_map/all_gather | solution.py:255
  571.9 28.5 %all-to-all-done.2 = bf16[1,256,3,8,128]{4,1,2,0,3:T(8,128)(2,1)} async-done(((bf16[1,256,3,8,128]{4,1,2,0,3:T(8,128)(2,1)}), bf16[1,256,3,8,128]{4,1,2,0,3:T(8,128)(2,1)}, u32[]{:S(2)}, u32[]{:S(2)}) %all-to-all-start.2) | async-done | bytes 1572896 | tf_op jit(solution)/shard_map/all_to_all | solution.py:269
  667.0 51.9 %all-gather.61.cloned.1.call-done = bf16[1,4096,1024]{2,1,0:T(8,128)(2,1)} async-done(((bf16[1,1024,1024]{2,1,0:T(8,128)(2,1)}), bf16[1,4096,1024]{2,1,0:T(8,128)(2,1)}) %all-gather.61.cloned.1.call-update) | async-done | bytes 8388624 | tf_op jit(solution)/shard_map/all_gather | solution.py:258
  750.4 26.7 %while.68 = (s32[]{:T(128)}, bf16[1,1024,2,128]{3,2,1,0:T(2,128)(2,1)}, f32[1,1024,2,128]{1,3,2,0:T(8,128)}, f32[1,1024,2,128]{1,3,2,0:T(8,128)}, s32[1]{0:T(128...) while((s32[]{:T(128)}, ...), condition=%wide.region_21.22_spmd.clone, body=%wide.region_19.21_spmd.clone.sunk | while | flops 1357382144 | bytes 88372160 | solution.py:202
  863.1 26.6 %while.69 = (s32[]{:T(128)}, bf16[1,1024,2,128]{3,2,1,0:T(2,128)(2,1)}, f32[1,1024,2,128]{1,3,2,0:T(8,128)}, f32[1,1024,2,128]{1,3,2,0:T(8,128)}, s32[1]{0:T(128...) while((s32[]{:T(128)}, ...), condition=%wide.region_28.29_spmd.clone, body=%wide.region_26.0_spmd.clone.sunk | while | flops 1357382144 | bytes 88372160 | solution.py:202
  991.7 61.6 %reduce-scatter.31.cloned.1.call-done = bf16[128,3,1024]{2,0,1:T(8,128)(2,1)} async-done(((bf16[1024,3,1024]{2,0,1:T(8,128)(2,1)}), bf16[128,3,1024]{2,0,1:T(8,128)(2,1)}) %reduce-scatter.31.cloned.1.call-update) | async-done | bytes 786448 | tf_op jit(solution)/shard_map/reduce_scatter | solution.py:82
  1053.4 120.9 %reduce-scatter.27.cloned.1.call-done = bf16[128,3,1024]{2,0,1:T(8,128)(2,1)} async-done(((bf16[1024,3,1024]{2,0,1:T(8,128)(2,1)}), bf16[128,3,1024]{2,0,1:T(8,128)(2,1)}) %reduce-scatter.27.cloned.1.call-update) | async-done | bytes 786448 | tf_op jit(solution)/shard_map/reduce_scatter | solution.py:82
  1174.4 151.7 %reduce-scatter.43.cloned.1.call-done = bf16[128,4096]{1,0:T(8,128)(2,1)} async-done(((bf16[1024,4096]{1,0:T(8,128)(2,1)}), bf16[128,4096]{1,0:T(8,128)(2,1)}) %reduce-scatter.43.cloned.1.call-update) | async-done | bytes 1048592 | tf_op jit(solution)/shard_map/reduce_scatter | solution.py:88
  1326.2 151.9 %reduce-scatter.39.cloned.1.call-done = bf16[128,4096]{1,0:T(8,128)(2,1)} async-done(((bf16[1024,4096]{1,0:T(8,128)(2,1)}), bf16[128,4096]{1,0:T(8,128)(2,1)}) %reduce-scatter.39.cloned.1.call-update) | async-done | bytes 1048592 | tf_op jit(solution)/shard_map/reduce_scatter | solution.py:88
  1478.2 151.7 %reduce-scatter.57.cloned.1.call-done = bf16[128,4096]{1,0:T(8,128)(2,1)} async-done(((bf16[1024,4096]{1,0:T(8,128)(2,1)}), bf16[128,4096]{1,0:T(8,128)(2,1)}) %reduce-scatter.57.cloned.1.call-update) | async-done | bytes 1048592
  1642.2 139.7 %reduce-scatter.55.cloned.1.call-done = bf16[128,4096]{1,0:T(8,128)(2,1)} async-done(((bf16[1024,4096]{1,0:T(8,128)(2,1)}), bf16[128,4096]{1,0:T(8,128)(2,1)}) %reduce-scatter.55.cloned.1.call-update) | async-done | bytes 1048592
  1789.4 35.8 %all-reduce.4 = (bf16[4,4,8,32]{3,0,2,1:T(4,128)(2,1)S(1)}, bf16[4,4,8,32]{3,0,2,1:T(4,128)(2,1)S(1)}) all-reduce(bf16[4,4,8,32]{3,0,2,1:T(4,128)(2,1)S(1)} %maximum_bitcast_fusion.1, bf16[4,4,8,32]{3,0,2,1:T(4,128)(2,1)S(1)} %maximum_bitcast_fusion), channel_id=40, replica_groups=mesh['dp'=8,'seq'=4] {'dp'}, use_global_device_ids=true, to_apply=%region_61.62.clone | all-reduce | flops 8192 | bytes 32768
  1906.2 27.6 %reduce-scatter.41.cloned.1.call-done = bf16[128,1024]{1,0:T(8,128)(2,1)} async-done(((bf16[128,4096]{1,0:T(8,128)(2,1)}), bf16[128,1024]{1,0:T(8,128)(2,1)}) %reduce-scatter.41.cloned.1.call-update) | async-done | bytes 262160 | tf_op jit(solution)/shard_map/reduce_scatter | solution.py:105
  1961.8 28.0 %reduce-scatter.47.cloned.1.call-done = bf16[1024,128]{1,0:T(8,128)(2,1)} async-done(((bf16[4096,128]{1,0:T(8,128)(2,1)}), bf16[1024,128]{1,0:T(8,128)(2,1)}) %reduce-scatter.47.cloned.1.call-update) | async-done | bytes 262160 | tf_op jit(solution)/shard_map/reduce_scatter | solution.py:108
  1995.3 39.5 %psum.7 = f32[]{:T(128)} all-reduce(f32[]{:T(128)S(6)} %add.592), channel_id=1, replica_groups=mesh['dp'=8,'seq'=4] {'dp','seq'}, use_global_device_ids=true, to_apply=%region_64.65 | all-reduce | flops 1 | bytes 8 | tf_op jit(solution)/shard_map/psum | solution.py:385
  (590 shorter events, 655.7 us)
Async XLA Ops:
  13.3 251.1 %all-gather.55.cloned.1.call-start = ((), (), s32[]{:S(2)}) async-start(), calls=%async_computation.46 | async-start | bytes 2359296 | tf_op jit(solution)/shard_map/all_gather | solution.py:66
  13.8 297.0 %all-gather.37.cloned.1.call-start = ((), (), s32[]{:S(2)}) async-start(), calls=%async_computation.37 | async-start | bytes 7864320 | tf_op jit(solution)/shard_map/all_gather | solution.py:255
  58.7 318.0 %all-gather.59.cloned.1.call-start = ((), (), s32[]{:S(2)}) async-start(), calls=%async_computation.48 | async-start | bytes 2359296 | tf_op jit(solution)/shard_map/all_gather | solution.py:67
  59.5 333.9 %all-gather.39.cloned.1.call-start = ((), (), s32[]{:S(2)}) async-start(), calls=%async_computation.38 | async-start | bytes 2621440 | tf_op jit(solution)/shard_map/all_gather | solution.py:256
  89.9 363.3 %all-gather.43.cloned.1.call-start = ((), (), s32[]{:S(2)}) async-start(), calls=%async_computation.40 | async-start | bytes 10485760 | tf_op jit(solution)/shard_map/all_gather | solution.py:257
  112.7 400.3 %all-gather.47.cloned.1.call-start = ((), (), s32[]{:S(2)}) async-start(), calls=%async_computation.42 | async-start | bytes 10485760 | tf_op jit(solution)/shard_map/all_gather | solution.py:258
  164.9 396.0 %all-gather.51.cloned.1.call-start = ((), (), s32[]{:S(2)}) async-start(), calls=%async_computation.44 | async-start | bytes 7864320 | tf_op jit(solution)/shard_map/all_gather | solution.py:255
  210.9 426.2 %all-gather.53.cloned.1.call-start = ((), (), s32[]{:S(2)}) async-start(), calls=%async_computation.45 | async-start | bytes 2621440 | tf_op jit(solution)/shard_map/all_gather | solution.py:256
  241.2 418.0 %all-gather.57.cloned.1.call-start = ((), (), s32[]{:S(2)}) async-start(), calls=%async_computation.47 | async-start | bytes 10485760 | tf_op jit(solution)/shard_map/all_gather | solution.py:257
  376.2 342.7 %all-gather.61.cloned.1.call-start = ((), (), s32[]{:S(2)}) async-start(), calls=%async_computation.49 | async-start | bytes 10485760 | tf_op jit(solution)/shard_map/all_gather | solution.py:258
  839.8 213.5 %reduce-scatter.31.cloned.1.call-start = ((), (), s32[]{:S(2)}) async-start(), calls=%async_computation.26 | async-start | bytes 7077888 | tf_op jit(solution)/shard_map/reduce_scatter | solution.py:82
  853.2 321.1 %reduce-scatter.27.cloned.1.call-start = ((), (), s32[]{:S(2)}) async-start(), calls=%async_computation.24 | async-start | bytes 7077888 | tf_op jit(solution)/shard_map/reduce_scatter | solution.py:82
  927.6 398.5 %reduce-scatter.43.cloned.1.call-start = ((), (), s32[]{:S(2)}) async-start(), calls=%async_computation.32 | async-start | bytes 9437184 | tf_op jit(solution)/shard_map/reduce_scatter | solution.py:88
  936.2 541.9 %reduce-scatter.39.cloned.1.call-start = ((), (), s32[]{:S(2)}) async-start(), calls=%async_computation.30 | async-start | bytes 9437184 | tf_op jit(solution)/shard_map/reduce_scatter | solution.py:88
  944.9 684.9 %reduce-scatter.57.cloned.1.call-start = ((), (), s32[]{:S(2)}) async-start(), calls=%async_computation.53 | async-start | bytes 9437184
  966.3 815.6 %reduce-scatter.55.cloned.1.call-start = ((), (), s32[]{:S(2)}) async-start(), calls=%async_computation.52 | async-start | bytes 9437184
  987.7 846.5 %reduce-scatter.37.cloned.1.call-start = ((), (), s32[]{:S(2)}) async-start(), calls=%async_computation.29 | async-start | bytes 327680 | tf_op jit(solution)/shard_map/reduce_scatter | solution.py:102
  989.8 844.5 %reduce-scatter.35.cloned.1.call-start = ((), (), s32[]{:S(2)}) async-start(), calls=%async_computation.28 | async-start | bytes 327680 | tf_op jit(solution)/shard_map/reduce_scatter | solution.py:102
  991.6 861.4 %reduce-scatter.33.cloned.1.call-start = ((), (), s32[]{:S(2)}) async-start(), calls=%async_computation.27 | async-start | bytes 983040 | tf_op jit(solution)/shard_map/reduce_scatter | solution.py:99
  1053.3 825.5 %reduce-scatter.29.cloned.1.call-start = ((), (), s32[]{:S(2)}) async-start(), calls=%async_computation.25 | async-start | bytes 983040 | tf_op jit(solution)/shard_map/reduce_scatter | solution.py:99
  1174.3 731.9 %reduce-scatter.45.cloned.1.call-start = ((), (), s32[]{:S(2)}) async-start(), calls=%async_computation.33 | async-start | bytes 1310720 | tf_op jit(solution)/shard_map/reduce_scatter | solution.py:105
  1326.1 607.6 %reduce-scatter.41.cloned.1.call-start = ((), (), s32[]{:S(2)}) async-start(), calls=%async_computation.31 | async-start | bytes 1310720 | tf_op jit(solution)/shard_map/reduce_scatter | solution.py:105
  1478.1 483.7 %reduce-scatter.49.cloned.1.call-start = ((), (), s32[]{:S(2)}) async-start(), calls=%async_computation.35 | async-start | bytes 1310720 | tf_op jit(solution)/shard_map/reduce_scatter | solution.py:108
  1632.1 357.7 %reduce-scatter.47.cloned.1.call-start = ((), (), s32[]{:S(2)}) async-start(), calls=%async_computation.34 | async-start | bytes 1310720 | tf_op jit(solution)/shard_map/reduce_scatter | solution.py:108
  (134 other events, 7453.2 us)
Sparse Core Ops, SparseCore 0:
  10.7 47.9 all-gather.34
  61.4 51.2 all-gather.40
  115.3 49.5 all-gather.44
  167.4 43.4 all-gather.48
  213.4 50.8 all-gather.54
  265.8 45.0 all-gather.36
  313.5 51.5 all-gather.58
  366.6 26.6 all-gather.38
  394.9 58.2 all-gather.42
  454.7 58.2 all-gather.46
  514.5 46.3 all-gather.50
  562.4 31.0 all-gather.52
  595.0 64.1 all-gather.56
  660.6 58.2 all-gather.60
  793.0 69.2 reduce-scatter.52
  865.6 66.8 reduce-scatter.50
  936.0 117.3 reduce-scatter.30
  1056.8 117.4 reduce-scatter.26
  1177.9 148.1 reduce-scatter.42
  1330.0 148.0 reduce-scatter.38
  1481.7 148.0 reduce-scatter.56
  1633.9 148.0 reduce-scatter.54
  1881.2 24.8 reduce-scatter.44
  1936.9 24.8 reduce-scatter.48
  (6 shorter events, 135.0 us)
where the time goes:
time: 2070 us; the launch traced here: 2060 us
  waiting for transfers between devices  1440 us (70%)
  blocking collectives  237 us (11%)
  matrix products  178 us (9%)
  local copies, waits for them, and re-layouts  95.6 us (5%)
  other arithmetic  57.9 us (3%)
  starting transfers between devices  29.1 us (1%)
  between operations  22.3 us (1%)
    reduce_scatter x2, waiting for transfers between devices, reduce_grads(): lax.psum_scatter(up_part.astype(jnp.bfloat16), 'dp', scatter_dimension=0,...  304 us
    unnamed x34, waiting for transfers between devices  294 us
    reduce_scatter x2, waiting for transfers between devices, reduce_grads(): lax.psum_scatter(qkv_part.astype(jnp.bfloat16), 'dp', scatter_dimension=0...  183 us
    all_gather x2, waiting for transfers between devices, body(): lax.all_gather(down_group, 'seq', axis=0, tiled=True)  104 us
    all_gather x2, waiting for transfers between devices, gather_groups(): lax.all_gather(qkv_part, 'dp', axis=0, tiled=True)  90.7 us
    all_gather x2, waiting for transfers between devices, body(): lax.all_gather(up_group, 'seq', axis=1, tiled=True)  76.1 us
    all_gather x2, blocking collectives, gather_groups(): lax.all_gather(norm_part, 'dp', axis=1, tiled=True)  61.5 us
    all_gather x2, blocking collectives, gather_groups(): lax.all_gather(proj_part, 'dp', axis=1, tiled=True)  60.6 us
  transfers between devices with their start and end apart: 37, of which 30 were waited for; matrix products, arithmetic and copies ran while one was open for 12% of the time, Pallas kernels for 0%

commit v1 on v0

--- a/solution.py
+++ b/solution.py
@@ -53,66 +53,25 @@
     return (grad_hidden, jnp.sum(grad_out * scaled, axis=0), jnp.sum(grad_out, axis=0))
 
 
-def gather_groups(masters, layer_index):
-    qkv_part = masters[0][layer_index].astype(jnp.bfloat16)
-    proj_part = masters[1][layer_index].astype(jnp.bfloat16)
-    up_part = masters[2][layer_index].astype(jnp.bfloat16)
-    down_part = masters[3][layer_index].astype(jnp.bfloat16)
-    norm_local = masters[4][layer_index].astype(jnp.bfloat16)
-    norm_part = norm_local.reshape(4, 1, norm_local.shape[1])
+def pack_layer(masters, layer_index):
+    qkv, proj, up, down = (masters[i][layer_index].astype(jnp.bfloat16) for i in range(4))
+    return qkv.reshape(qkv.shape[0], -1), proj, up, down
+
+
+def gather_layer(masters, layer_index):
+    qkv, proj, up, down = pack_layer(masters, layer_index)
     return (
-        lax.all_gather(qkv_part, "dp", axis=0, tiled=True),
-        lax.all_gather(proj_part, "dp", axis=1, tiled=True),
-        lax.all_gather(up_part, "dp", axis=0, tiled=True),
-        lax.all_gather(down_part, "dp", axis=1, tiled=True),
-        lax.all_gather(norm_part, "dp", axis=1, tiled=True),
-    )
-
-
-def order_norm(norm_every):
-    return jnp.transpose(norm_every, (1, 2, 0, 3)).reshape(4, -1).astype(jnp.float32)
-
-
-def reduce_grads(qkv_part, proj_part, up_part, down_part, norm_part):
-    group_count = lax.axis_size("dp")
-    seq_count = lax.axis_size("seq")
-    piece = norm_part.shape[1] // (group_count * seq_count)
-    arranged = jnp.transpose(norm_part.reshape(4, group_count, seq_count, piece), (2, 0, 1, 3))
-    group_qkv, group_proj, group_up, group_down, group_norm = (
-        lax.psum_scatter(
-            qkv_part.astype(jnp.bfloat16), "dp", scatter_dimension=0, tiled=True
-        ).astype(jnp.float32),
-        lax.psum_scatter(
-            proj_part.astype(jnp.bfloat16), "dp", scatter_dimension=1, tiled=True
-        ).astype(jnp.float32),
-        lax.psum_scatter(
-            up_part.astype(jnp.bfloat16), "dp", scatter_dimension=0, tiled=True
-        ).astype(jnp.float32),
-        lax.psum_scatter(
-            down_part.astype(jnp.bfloat16), "dp", scatter_dimension=1, tiled=True
-        ).astype(jnp.float32),
-        lax.psum_scatter(
-            arranged.astype(jnp.bfloat16), "dp", scatter_dimension=2, tiled=True
-        ).astype(jnp.float32),
-    )
-    final_qkv, final_proj, final_up, final_down, final_norm = (
-        lax.psum_scatter(
-            group_qkv.astype(jnp.bfloat16), "seq", scatter_dimension=2, tiled=True
-        ).astype(jnp.float32),
-        lax.psum_scatter(
-            group_proj.astype(jnp.bfloat16), "seq", scatter_dimension=0, tiled=True
-        ).astype(jnp.float32),
-        lax.psum_scatter(
-            group_up.astype(jnp.bfloat16), "seq", scatter_dimension=1, tiled=True
-        ).astype(jnp.float32),
-        lax.psum_scatter(
-            group_down.astype(jnp.bfloat16), "seq", scatter_dimension=0, tiled=True
-        ).astype(jnp.float32),
-        lax.psum_scatter(
-            group_norm.astype(jnp.bfloat16), "seq", scatter_dimension=0, tiled=True
-        ).astype(jnp.float32),
-    )
-    return (final_qkv, final_proj, final_up, final_down, final_norm.reshape(4, piece))
+        lax.all_gather(qkv, "dp", axis=0, tiled=True),
+        lax.all_gather(proj, "dp", axis=1, tiled=True),
+        lax.all_gather(up, "dp", axis=0, tiled=True),
+        lax.all_gather(down, "dp", axis=1, tiled=True),
+    )
+
+
+def scatter_sum(part, axis_name, dimension):
+    return lax.psum_scatter(
+        part.astype(jnp.bfloat16), axis_name, scatter_dimension=dimension, tiled=True
+    ).astype(jnp.float32)
 
 
 def block_scores(query_block, key_rows, first_row, slopes, lengths):
@@ -246,51 +205,39 @@
         axis=1,
     )
     hidden = block_input.astype(jnp.float32).reshape(token_count, model_width)
+    local_width = head_local * HD
+    group_count = lax.axis_size("dp")
+    norm_piece = norm_params.shape[2]
+    norm_all = lax.all_gather(
+        norm_params.astype(jnp.bfloat16), ("dp", "seq"), axis=2, tiled=True
+    ).astype(jnp.float32)
     saved = []
     for layer_index in range(layer_count):
-        qkv_group, proj_group, up_group, down_group, norm_group = gather_groups(
-            masters, layer_index
-        )
-        qkv_all, w_proj, w_up, w_down, norm_every = (
-            lax.all_gather(qkv_group, "seq", axis=2, tiled=True),
-            lax.all_gather(proj_group, "seq", axis=0, tiled=True),
-            lax.all_gather(up_group, "seq", axis=1, tiled=True),
-            lax.all_gather(down_group, "seq", axis=0, tiled=True),
-            lax.all_gather(norm_group[None], "seq", axis=0, tiled=True),
-        )
-        w_qkv = qkv_all.reshape(model_width, -1)
-        norm_rows = order_norm(norm_every)
+        w_qkv, w_proj, w_up, w_down = gather_layer(masters, layer_index)
+        norm_rows = norm_all[layer_index]
         unused, normed = layer_norm(hidden, norm_rows[0], norm_rows[1])
-        normed_low = normed.astype(jnp.bfloat16)
-        projected = jnp.dot(normed_low, w_qkv, preferred_element_type=jnp.float32).astype(
+        normed_one = lax.all_gather(normed.astype(jnp.bfloat16), "seq", axis=0, tiled=True)
+        projected = jnp.dot(normed_one, w_qkv, preferred_element_type=jnp.float32).astype(
             jnp.bfloat16
         )
-        projected = projected.reshape(row_count, local_slots, 3, H, HD)
-        spread = lax.all_to_all(projected, "seq", split_axis=3, concat_axis=1, tiled=True)
+        spread = projected.reshape(row_count, local_slots * seq_count, 3, head_local, HD)
         context, log_total = attend_forward(
             spread[:, :, 0], spread[:, :, 1], spread[:, :, 2], slopes, row_lengths
         )
-        context_tokens = lax.all_to_all(
-            context, "seq", split_axis=1, concat_axis=2, tiled=True
-        ).reshape(token_count, model_width)
-        middle = hidden + jnp.dot(context_tokens, w_proj, preferred_element_type=jnp.float32)
+        context_rows = context.reshape(-1, local_width)
+        middle = hidden + scatter_sum(
+            jnp.dot(context_rows, w_proj, preferred_element_type=jnp.float32), "seq", 0
+        )
         unused, normed_two = layer_norm(middle, norm_rows[2], norm_rows[3])
-        upper = jnp.dot(normed_two.astype(jnp.bfloat16), w_up, preferred_element_type=jnp.float32)
+        normed_two = lax.all_gather(normed_two.astype(jnp.bfloat16), "seq", axis=0, tiled=True)
+        upper = jnp.dot(normed_two, w_up, preferred_element_type=jnp.float32)
         act_low = smooth_act(upper).astype(jnp.bfloat16)
-        following = middle + jnp.dot(act_low, w_down, preferred_element_type=jnp.float32)
+        following = middle + scatter_sum(
+            jnp.dot(act_low, w_down, preferred_element_type=jnp.float32), "seq", 0
+        )
         saved.append(
-            (
-                hidden,
-                middle,
-                spread,
-                log_total,
-                context_tokens,
-                act_low,
-                upper,
-                normed_low,
-                None,
-                (w_qkv, w_proj, w_up, w_down, norm_rows),
-            )
+            (hidden, middle, spread, log_total, context_rows, act_low, upper, normed_one,
+             normed_two, (w_qkv, w_proj, w_up, w_down, norm_rows))
         )
         hidden = following
     block_output = hidden.reshape(row_count, local_slots, model_width)
@@ -300,81 +247,62 @@
         token_count, model_width
     )
     reduced_all = [None] * layer_count
+    norm_parts = [None] * layer_count
     for layer_index in reversed(range(layer_count)):
-        (
-            hidden_in,
-            middle,
-            spread,
-            log_total,
-            context_saved,
-            act_low,
-            upper,
-            normed_kept,
-            normed_two_kept,
-            weights,
-        ) = saved[layer_index]
+        (hidden_in, middle, spread, log_total, context_rows, act_low, upper, normed_one,
+         normed_two, weights) = saved[layer_index]
         w_qkv, w_proj, w_up, w_down, norm_rows = weights
-        grad_ffn = grad_hidden.astype(jnp.bfloat16)
-        unused, normed_two = layer_norm(middle, norm_rows[2], norm_rows[3])
-        down_grad = jnp.einsum("tf,td->fd", act_low, grad_ffn, preferred_element_type=jnp.float32)
+        grad_ffn = lax.all_gather(grad_hidden.astype(jnp.bfloat16), "seq", axis=0, tiled=True)
+        down_grad = scatter_sum(
+            jnp.einsum("tf,td->fd", act_low, grad_ffn, preferred_element_type=jnp.float32), "dp", 1
+        )
         grad_act = jnp.einsum("td,fd->tf", grad_ffn, w_down, preferred_element_type=jnp.float32)
         grad_upper = smooth_back(upper, grad_act).astype(jnp.bfloat16)
-        up_grad = jnp.einsum(
-            "td,tf->df",
-            normed_two.astype(jnp.bfloat16),
-            grad_upper,
-            preferred_element_type=jnp.float32,
-        )
-        grad_normed_two = jnp.einsum(
-            "tf,df->td", grad_upper, w_up, preferred_element_type=jnp.float32
+        up_grad = scatter_sum(
+            jnp.einsum("td,tf->df", normed_two, grad_upper, preferred_element_type=jnp.float32),
+            "dp", 0,
+        )
+        grad_normed_two = scatter_sum(
+            jnp.einsum("tf,df->td", grad_upper, w_up, preferred_element_type=jnp.float32), "seq", 0
         )
         grad_middle_norm, gain_two, bias_two = norm_back(middle, norm_rows[2], grad_normed_two)
         grad_middle = grad_hidden + grad_middle_norm
-        grad_branch = grad_middle.astype(jnp.bfloat16)
-        proj_grad = jnp.einsum(
-            "td,te->de", context_saved, grad_branch, preferred_element_type=jnp.float32
+        grad_branch = lax.all_gather(grad_middle.astype(jnp.bfloat16), "seq", axis=0, tiled=True)
+        proj_grad = scatter_sum(
+            jnp.einsum("td,te->de", context_rows, grad_branch, preferred_element_type=jnp.float32),
+            "dp", 1,
         )
         grad_context = jnp.einsum(
             "te,de->td", grad_branch, w_proj, preferred_element_type=jnp.float32
         ).astype(jnp.bfloat16)
-        grad_context = lax.all_to_all(
-            grad_context.reshape(row_count, local_slots, H, HD),
-            "seq",
-            split_axis=2,
-            concat_axis=1,
-            tiled=True,
-        )
+        grad_context = grad_context.reshape(row_count, -1, head_local, HD)
         grad_queries, grad_keys, grad_values = attend_backward(
-            spread[:, :, 0],
-            spread[:, :, 1],
-            spread[:, :, 2],
-            grad_context,
-            log_total,
-            slopes,
+            spread[:, :, 0], spread[:, :, 1], spread[:, :, 2], grad_context, log_total, slopes,
             row_lengths,
         )
-        grad_spread = jnp.stack(
+        grad_projected = jnp.stack(
             (grad_queries, grad_keys.astype(jnp.bfloat16), grad_values.astype(jnp.bfloat16)), axis=2
-        )
-        grad_projected = lax.all_to_all(
-            grad_spread, "seq", split_axis=1, concat_axis=3, tiled=True
-        ).reshape(token_count, 3 * model_width)
-        qkv_grad = jnp.einsum(
-            "td,te->de", normed_kept, grad_projected, preferred_element_type=jnp.float32
-        )
-        qkv_grad = qkv_grad.reshape(model_width, 3, model_width)
-        grad_normed = jnp.einsum(
-            "te,de->td", grad_projected, w_qkv, preferred_element_type=jnp.float32
+        ).reshape(-1, 3 * local_width)
+        qkv_grad = scatter_sum(
+            jnp.einsum("td,te->de", normed_one, grad_projected, preferred_element_type=jnp.float32),
+            "dp", 0,
+        ).reshape(-1, 3, local_width)
+        grad_normed = scatter_sum(
+            jnp.einsum("te,de->td", grad_projected, w_qkv, preferred_element_type=jnp.float32),
+            "seq", 0,
         )
         grad_input_norm, gain_one, bias_one = norm_back(hidden_in, norm_rows[0], grad_normed)
         grad_hidden = grad_middle + grad_input_norm
-        norm_grad = jnp.stack((gain_one, bias_one, gain_two, bias_two), axis=0)
-        reduced_all[layer_index] = reduce_grads(qkv_grad, proj_grad, up_grad, down_grad, norm_grad)
+        norm_parts[layer_index] = jnp.stack((gain_one, bias_one, gain_two, bias_two), axis=0)
+        reduced_all[layer_index] = (qkv_grad, proj_grad, up_grad, down_grad)
     input_grad = grad_hidden.reshape(row_count, local_slots, model_width)
+    norm_grad = lax.psum_scatter(
+        jnp.stack(norm_parts, axis=0), ("dp", "seq"), scatter_dimension=2, tiled=True
+    )
     stacked = [
         jnp.stack([layer_grads[position] for layer_grads in reduced_all], axis=0)
-        for position in range(5)
-    ]
+        for position in range(4)
+    ] + [norm_grad]
     square_sum = (
         jnp.sum(stacked[0] * stacked[0])
         + jnp.sum(stacked[1] * stacked[1])

time: 2070 us -> 1690 us (0.82)
  waiting for transfers between devices: 1440 us -> 1180 us
  blocking collectives: 237 us -> 142 us
  starting transfers between devices: 29.1 us -> 3.11 us
  matrix products: 178 us -> 155 us
    reduce_scatter x12, waiting for transfers between devices: 632 us -> 499 us  [scatter_sum(): lax.psum_scatter(part.astype(jnp.bfloat16), axis_name, scatter_dimension=...]
    all_to_all x7 -> x0, waiting for transfers between devices: 89.5 us -> none  [the longest x2 28.5 us: body(): lax.all_to_all(projected, 'seq', split_axis=3, concat_axis=1, tiled=True)]
    all_gather x14, waiting for transfers between devices: 420 us -> 343 us  [the longest x2 101 us: gather_layer(): lax.all_gather(down, 'dp', axis=1, tiled=True)]
    unnamed x34 -> x36, waiting for transfers between devices: 294 us -> 343 us
    unnamed x2 -> x0, blocking collectives: 41.6 us -> none
    all_gather x6 -> x3, blocking collectives: 133 us -> 105 us  [the longest x2 59.6 us: gather_layer(): lax.all_gather(proj, 'dp', axis=1, tiled=True)]
    slice x6 -> x1, local copies, waits for them, and re-layouts: 0.04 us -> 27.2 us  [body(): unused, normed_two = layer_norm(middle, norm_rows[2], norm_rows[3])]
    all_to_all x7 -> x0, starting transfers between devices: 26.8 us -> none  [the longest x2 7.95 us: body(): lax.all_to_all(projected, 'seq', split_axis=3, concat_axis=1, tiled=True)]
  transfers between devices with their start and end apart: 37 -> 31, of which waited for: 30 -> 28; matrix products, arithmetic and copies ran while one was open for 12% -> 10% of each run, Pallas kernels for 0% -> 0%
where the time goes in v1:
time: 1690 us; the launch traced here: 1680 us
  waiting for transfers between devices  1180 us (70%)
  matrix products  155 us (9%)
  blocking collectives  142 us (8%)
  local copies, waits for them, and re-layouts  92.4 us (5%)
  other arithmetic  78.4 us (5%)
  between operations  21.7 us (1%)
    reduce_scatter x12, waiting for transfers between devices, scatter_sum(): lax.psum_scatter(part.astype(jnp.bfloat16), axis_name, scatter_dimension=...  499 us
    unnamed x36, waiting for transfers between devices  343 us
    all_gather x2, waiting for transfers between devices, gather_layer(): lax.all_gather(down, 'dp', axis=1, tiled=True)  101 us
    all_gather x2, waiting for transfers between devices, gather_layer(): lax.all_gather(up, 'dp', axis=0, tiled=True)  92.2 us
    all_gather x2, blocking collectives, gather_layer(): lax.all_gather(proj, 'dp', axis=1, tiled=True)  59.6 us
    all_gather x2, waiting for transfers between devices, body(): lax.all_gather(normed_two.astype(jnp.bfloat16), 'seq', axis=0, tiled=True)  46.4 us
    all_gather x1, blocking collectives, body(): lax.all_gather(norm_params.astype(jnp.bfloat16), ('dp', 'seq'), axis=2, t...  45.5 us
    all_gather x2, waiting for transfers between devices, body(): lax.all_gather(grad_hidden.astype(jnp.bfloat16), 'seq', axis=0, tiled=True)  40.6 us
  transfers between devices with their start and end apart: 31, of which 28 were waited for; matrix products, arithmetic and copies ran while one was open for 10% of the time, Pallas kernels for 0%

profile of v1, /device:TPU:0, one launch (start us, length us, event | category | flops | bytes accessed | tf_op | source)
XLA Modules:
  0.0 1677.9 jit_solution(130323441851909933)
XLA Ops:
  10.6 45.5 %all_gather.51 = bf16[2,4,1024]{1,0,2:T(2,128)(2,1)S(1)} all-gather(bf16[2,4,32]{1,0,2:T(2,128)(2,1)S(1)} %copy.182), channel_id=1, replica_groups=mesh['dp'=8,'seq'=4] {'dp','seq'}, dimensions={2}, use_global_device_ids=true | all-gather | bytes 16896 | tf_op jit(solution)/shard_map/all_gather | solution.py:211
  56.9 27.2 %slice_reduce_fusion.1 = (f32[1024]{0:T(1024)S(1)}, f32[1024]{0:T(1024)S(1)}, f32[1024]{0:T(1024)S(1)}, f32[1024]{0:T(1024)S(1)}, f32[1024]{0:T(1024)S(1)}, /*in...) fusion(f32[2,4,1024]{1,0,2:T(2,128)S(1)} %convert_element_type.368), kind=kLoop, calls=%fused_computation.271 | loop fusion | bytes 65536 | tf_op jit(solution)/shard_map/slice | solution.py:231
  86.1 29.0 %all-gather = bf16[1,256,1024]{2,1,0:T(8,128)(2,1)} all-gather(bf16[1,256,128]{2,1,0:T(8,128)(2,1)S(1)} %get-tuple-element.1191), channel_id=2, replica_groups=mesh['dp'=8,'seq'=4] {'dp'}, dimensions={2}, use_global_device_ids=true | all-gather | bytes 589824 | tf_op jit(solution)/shard_map/all_gather | solution.py:65
  139.2 27.4 %reduce-scatter.28.cloned.1.call-done = bf16[256,1024]{1,0:T(8,128)(2,1)} async-done(((bf16[1024,1024]{1,0:T(8,128)(2,1)}), bf16[256,1024]{1,0:T(8,128)(2,1)}) %reduce-scatter.28.cloned.1.call-update) | async-done | bytes 524304 | tf_op jit(solution)/shard_map/reduce_scatter | solution.py:72
  172.9 45.8 %all-gather.41.cloned.1.call-done = bf16[1,1024,1024]{2,1,0:T(8,128)(2,1)} async-done(((bf16[1,128,1024]{2,1,0:T(8,128)(2,1)}), bf16[1,1024,1024]{2,1,0:T(8,128)(2,1)}) %all-gather.41.cloned.1.call-update) | async-done | bytes 2097168 | tf_op jit(solution)/shard_map/all_gather | solution.py:66
  248.4 47.3 %all-gather.43.cloned.1.call-done = bf16[1,1024,1024]{2,1,0:T(8,128)(2,1)} async-done(((bf16[1,1024,128]{2,1,0:T(8,128)(2,1)}), bf16[1,1024,1024]{2,1,0:T(8,128)(2,1)}) %all-gather.43.cloned.1.call-update) | async-done | bytes 2097168 | tf_op jit(solution)/shard_map/all_gather | solution.py:67
  303.3 29.0 %reduce-scatter.30.cloned.1.call-done = bf16[256,1024]{1,0:T(8,128)(2,1)} async-done(((bf16[1024,1024]{1,0:T(8,128)(2,1)}), bf16[256,1024]{1,0:T(8,128)(2,1)}) %reduce-scatter.30.cloned.1.call-update) | async-done | bytes 524304 | tf_op jit(solution)/shard_map/reduce_scatter | solution.py:72
  335.0 30.6 %all-gather.3 = bf16[1,256,1024]{2,1,0:T(8,128)(2,1)} all-gather(bf16[1,256,128]{2,1,0:T(8,128)(2,1)S(1)} %get-tuple-element.1190), channel_id=5, replica_groups=mesh['dp'=8,'seq'=4] {'dp'}, dimensions={2}, use_global_device_ids=true | all-gather | bytes 589824 | tf_op jit(solution)/shard_map/all_gather | solution.py:65
  429.4 30.6 %reduce-scatter.32.cloned.1.call-done = bf16[256,1024]{1,0:T(8,128)(2,1)} async-done(((bf16[1024,1024]{1,0:T(8,128)(2,1)}), bf16[256,1024]{1,0:T(8,128)(2,1)}) %reduce-scatter.32.cloned.1.call-update) | async-done | bytes 524304 | tf_op jit(solution)/shard_map/reduce_scatter | solution.py:72
  466.0 46.3 %all-gather.45.cloned.1.call-done = bf16[1,1024,1024]{2,1,0:T(8,128)(2,1)} async-done(((bf16[1,128,1024]{2,1,0:T(8,128)(2,1)}), bf16[1,1024,1024]{2,1,0:T(8,128)(2,1)}) %all-gather.45.cloned.1.call-update) | async-done | bytes 2097168 | tf_op jit(solution)/shard_map/all_gather | solution.py:66
  560.3 53.8 %all-gather.47.cloned.1.call-done = bf16[1,1024,1024]{2,1,0:T(8,128)(2,1)} async-done(((bf16[1,1024,128]{2,1,0:T(8,128)(2,1)}), bf16[1,1024,1024]{2,1,0:T(8,128)(2,1)}) %all-gather.47.cloned.1.call-update) | async-done | bytes 2097168 | tf_op jit(solution)/shard_map/all_gather | solution.py:67
  659.3 31.6 %reduce-scatter.34.cloned.1.call-done = bf16[256,1024]{1,0:T(8,128)(2,1)} async-done(((bf16[1024,1024]{1,0:T(8,128)(2,1)}), bf16[256,1024]{1,0:T(8,128)(2,1)}) %reduce-scatter.34.cloned.1.call-update) | async-done | bytes 524304 | tf_op jit(solution)/shard_map/reduce_scatter | solution.py:72
  752.3 31.5 %reduce-scatter.38.cloned.1.call-done = bf16[256,1024]{1,0:T(8,128)(2,1)} async-done(((bf16[1024,1024]{1,0:T(8,128)(2,1)}), bf16[256,1024]{1,0:T(8,128)(2,1)}) %reduce-scatter.38.cloned.1.call-update) | async-done | bytes 524304 | tf_op jit(solution)/shard_map/reduce_scatter | solution.py:72
  825.2 31.5 %reduce-scatter.40.cloned.1.call-done = bf16[256,1024]{1,0:T(8,128)(2,1)} async-done(((bf16[1024,1024]{1,0:T(8,128)(2,1)}), bf16[256,1024]{1,0:T(8,128)(2,1)}) %reduce-scatter.40.cloned.1.call-update) | async-done | bytes 524304 | tf_op jit(solution)/shard_map/reduce_scatter | solution.py:72
  956.6 64.1 %reduce-scatter.54.cloned.1.call-done = bf16[128,256]{1,0:T(8,128)(2,1)} async-done(((bf16[1024,256]{1,0:T(8,128)(2,1)}), bf16[128,256]{1,0:T(8,128)(2,1)}) %reduce-scatter.54.cloned.1.call-update) | async-done | bytes 65552
  1021.6 66.1 %reduce-scatter.46.cloned.1.call-done = bf16[128,768]{1,0:T(8,128)(2,1)} async-done(((bf16[1024,768]{1,0:T(8,128)(2,1)}), bf16[128,768]{1,0:T(8,128)(2,1)}) %reduce-scatter.46.cloned.1.call-update) | async-done | bytes 196624 | tf_op jit(solution)/shard_map/reduce_scatter | solution.py:72
  1088.9 69.3 %reduce-scatter.56.cloned.1.call-done = bf16[128,1024]{1,0:T(8,128)(2,1)} async-done(((bf16[1024,1024]{1,0:T(8,128)(2,1)}), bf16[128,1024]{1,0:T(8,128)(2,1)}) %reduce-scatter.56.cloned.1.call-update) | async-done | bytes 262160
  1160.2 68.5 %reduce-scatter.50.cloned.1.call-done = bf16[128,1024]{1,0:T(8,128)(2,1)} async-done(((bf16[1024,1024]{1,0:T(8,128)(2,1)}), bf16[128,1024]{1,0:T(8,128)(2,1)}) %reduce-scatter.50.cloned.1.call-update) | async-done | bytes 262160 | tf_op jit(solution)/shard_map/reduce_scatter | solution.py:72
  1228.7 70.4 %reduce-scatter.48.cloned.1.call-done = bf16[128,1024]{1,0:T(8,128)(2,1)} async-done(((bf16[1024,1024]{1,0:T(8,128)(2,1)}), bf16[128,1024]{1,0:T(8,128)(2,1)}) %reduce-scatter.48.cloned.1.call-update) | async-done | bytes 262160 | tf_op jit(solution)/shard_map/reduce_scatter | solution.py:72
  1301.0 63.2 %reduce-scatter.52.cloned.1.call-done = bf16[128,256]{1,0:T(8,128)(2,1)} async-done(((bf16[1024,256]{1,0:T(8,128)(2,1)}), bf16[128,256]{1,0:T(8,128)(2,1)}) %reduce-scatter.52.cloned.1.call-update) | async-done | bytes 65552
  1366.4 65.1 %reduce-scatter.44.cloned.1.call-done = bf16[128,768]{1,0:T(8,128)(2,1)} async-done(((bf16[1024,768]{1,0:T(8,128)(2,1)}), bf16[128,768]{1,0:T(8,128)(2,1)}) %reduce-scatter.44.cloned.1.call-update) | async-done | bytes 196624 | tf_op jit(solution)/shard_map/reduce_scatter | solution.py:72
  1440.4 24.1 %reduce-scatter.42.cloned.1.call-done = bf16[256,1024]{1,0:T(8,128)(2,1)} async-done(((bf16[1024,1024]{1,0:T(8,128)(2,1)}), bf16[256,1024]{1,0:T(8,128)(2,1)}) %reduce-scatter.42.cloned.1.call-update) | async-done | bytes 524304 | tf_op jit(solution)/shard_map/reduce_scatter | solution.py:72
  1470.1 133.9 %reduce-scatter.60.cloned.1.call-done = f32[32,8]{1,0:T(8,128)} async-done(((f32[1024,8]{1,0:T(8,128)}), f32[32,8]{1,0:T(8,128)}) %reduce-scatter.60.cloned.1.call-update) | async-done | bytes 1040
  1608.9 36.8 %psum.7 = f32[]{:T(128)} all-reduce(f32[]{:T(128)S(6)} %add.574), channel_id=1, replica_groups=mesh['dp'=8,'seq'=4] {'dp','seq'}, use_global_device_ids=true, to_apply=%region_61.62 | all-reduce | flops 1 | bytes 8 | tf_op jit(solution)/shard_map/psum | solution.py:313
  (462 shorter events, 561.3 us)
Async XLA Ops:
  7.2 107.9 %all-gather.23.cloned.1.call-start = ((), (), s32[]{:S(2)}) async-start(), calls=%async_computation.18 | async-start | bytes 1769472 | tf_op jit(solution)/shard_map/all_gather | solution.py:64
  9.7 105.4 %all-gather.21.cloned.1.call-start = ((), (), s32[]{:S(2)}) async-start(), calls=%async_computation.17 | async-start | bytes 2621440 | tf_op jit(solution)/shard_map/all_gather | solution.py:219
  139.1 102.7 %all-gather.25.cloned.1.call-start = ((), (), s32[]{:S(2)}) async-start(), calls=%async_computation.20 | async-start | bytes 2621440 | tf_op jit(solution)/shard_map/all_gather | solution.py:232
  171.4 124.2 %all-gather.43.cloned.1.call-start = ((), (), s32[]{:S(2)}) async-start(), calls=%async_computation.40 | async-start | bytes 2359296 | tf_op jit(solution)/shard_map/all_gather | solution.py:67
  172.4 159.9 %reduce-scatter.30.cloned.1.call-start = ((), (), s32[]{:S(2)}) async-start(), calls=%async_computation.21 | async-start | bytes 2621440 | tf_op jit(solution)/shard_map/reduce_scatter | solution.py:72
  303.3 102.6 %all-gather.27.cloned.1.call-start = ((), (), s32[]{:S(2)}) async-start(), calls=%async_computation.22 | async-start | bytes 2621440 | tf_op jit(solution)/shard_map/all_gather | solution.py:219
  335.0 125.1 %reduce-scatter.32.cloned.1.call-start = ((), (), s32[]{:S(2)}) async-start(), calls=%async_computation.24 | async-start | bytes 2621440 | tf_op jit(solution)/shard_map/reduce_scatter | solution.py:72
  428.5 83.8 %all-gather.45.cloned.1.call-start = ((), (), s32[]{:S(2)}) async-start(), calls=%async_computation.41 | async-start | bytes 2359296 | tf_op jit(solution)/shard_map/all_gather | solution.py:66
  429.2 106.3 %all-gather.31.cloned.1.call-start = ((), (), s32[]{:S(2)}) async-start(), calls=%async_computation.25 | async-start | bytes 2621440 | tf_op jit(solution)/shard_map/all_gather | solution.py:232
  462.6 97.7 %all-gather.33.cloned.1.call-start = ((), (), s32[]{:S(2)}) async-start(), calls=%async_computation.27 | async-start | bytes 2621440 | tf_op jit(solution)/shard_map/all_gather | solution.py:255
  465.3 148.8 %all-gather.47.cloned.1.call-start = ((), (), s32[]{:S(2)}) async-start(), calls=%async_computation.42 | async-start | bytes 2359296 | tf_op jit(solution)/shard_map/all_gather | solution.py:67
  465.9 191.2 %reduce-scatter.36.cloned.1.call-start = ((), (), s32[]{:S(2)}) async-start(), calls=%async_computation.28 | async-start | bytes 2621440 | tf_op jit(solution)/shard_map/reduce_scatter | solution.py:72
  634.2 82.8 %all-gather.35.cloned.1.call-start = ((), (), s32[]{:S(2)}) async-start(), calls=%async_computation.29 | async-start | bytes 2621440 | tf_op jit(solution)/shard_map/all_gather | solution.py:270
  694.3 89.5 %reduce-scatter.38.cloned.1.call-start = ((), (), s32[]{:S(2)}) async-start(), calls=%async_computation.30 | async-start | bytes 2621440 | tf_op jit(solution)/shard_map/reduce_scatter | solution.py:72
  861.1 94.3 %reduce-scatter.58.cloned.1.call-start = ((), (), s32[]{:S(2)}) async-start(), calls=%async_computation.46 | async-start | bytes 2359296
  869.3 151.3 %reduce-scatter.54.cloned.1.call-start = ((), (), s32[]{:S(2)}) async-start(), calls=%async_computation.44 | async-start | bytes 589824
  872.8 214.9 %reduce-scatter.46.cloned.1.call-start = ((), (), s32[]{:S(2)}) async-start(), calls=%async_computation.36 | async-start | bytes 1769472 | tf_op jit(solution)/shard_map/reduce_scatter | solution.py:72
  877.7 280.5 %reduce-scatter.56.cloned.1.call-start = ((), (), s32[]{:S(2)}) async-start(), calls=%async_computation.45 | async-start | bytes 2359296
  886.1 342.6 %reduce-scatter.50.cloned.1.call-start = ((), (), s32[]{:S(2)}) async-start(), calls=%async_computation.38 | async-start | bytes 2359296 | tf_op jit(solution)/shard_map/reduce_scatter | solution.py:72
  892.1 407.0 %reduce-scatter.48.cloned.1.call-start = ((), (), s32[]{:S(2)}) async-start(), calls=%async_computation.37 | async-start | bytes 2359296 | tf_op jit(solution)/shard_map/reduce_scatter | solution.py:72
  898.1 466.0 %reduce-scatter.52.cloned.1.call-start = ((), (), s32[]{:S(2)}) async-start(), calls=%async_computation.43 | async-start | bytes 589824
  931.7 499.9 %reduce-scatter.44.cloned.1.call-start = ((), (), s32[]{:S(2)}) async-start(), calls=%async_computation.35 | async-start | bytes 1769472 | tf_op jit(solution)/shard_map/reduce_scatter | solution.py:72
  937.6 526.9 %reduce-scatter.42.cloned.1.call-start = ((), (), s32[]{:S(2)}) async-start(), calls=%async_computation.34 | async-start | bytes 2621440 | tf_op jit(solution)/shard_map/reduce_scatter | solution.py:72
  942.4 661.7 %reduce-scatter.60.cloned.1.call-start = ((), (), s32[]{:S(2)}) async-start(), calls=%async_computation.47 | async-start | bytes 540672
  (82 other events, 5484.2 us)
Sparse Core Ops, SparseCore 0:
  10.7 48.3 all-gather.22
  138.2 28.3 reduce-scatter.27
  169.4 49.2 all-gather.40
  244.5 51.0 all-gather.42
  302.6 29.6 reduce-scatter.29
  334.9 47.9 all-gather.28
  428.6 31.4 reduce-scatter.31
  463.0 49.2 all-gather.44
  563.0 51.0 all-gather.46
  627.4 29.6 reduce-scatter.35
  659.5 31.3 reduce-scatter.33
  752.4 31.3 reduce-scatter.37
  825.3 31.4 reduce-scatter.39
  861.2 22.5 all-gather.38
  887.8 67.5 reduce-scatter.57
  959.7 60.8 reduce-scatter.53
  1023.9 63.7 reduce-scatter.45
  1091.7 66.4 reduce-scatter.55
  1162.0 66.6 reduce-scatter.49
  1232.5 66.5 reduce-scatter.47
  1303.4 60.7 reduce-scatter.51
  1367.6 63.9 reduce-scatter.43
  1434.1 30.3 reduce-scatter.41
  1470.2 133.7 reduce-scatter.59
  (7 shorter events, 149.0 us)

commit v2 on v1

--- a/solution.py
+++ b/solution.py
@@ -1,13 +1,18 @@
+import functools
+
 import jax
 import jax.numpy as jnp
 import numpy as np
 from jax import lax
+from jax.experimental import pallas as pl
+from jax.experimental.pallas import tpu as pltpu
 from jax.sharding import PartitionSpec as P
 
 H = 8
 HD = 128
 STEP = 5
-
+CORES = 2
+ZSIZE = 4
 
 EPS_NORM = 1e-05
 BETA_ONE = 0.5
@@ -18,26 +23,582 @@
 CLIP_NORM = 0.1
 ADAM_EPS = 1e-08
 
+F32 = jnp.float32
+BF16 = jnp.bfloat16
+MESH = pl.DeviceIdType.MESH
+SCORE_SCALE = HD ** (-0.5)
+GELU_A = (2.0 / np.pi) ** 0.5
+GELU_B = 0.044715
+
 
 def slope_table(head_count):
     return np.power(2.0, -8.0 * (np.arange(head_count) + 1.0) / head_count)
 
 
-def smooth_act(values):
-    return jax.nn.gelu(values, approximate=True)
-
-
-def smooth_back(upper, grad_act):
-    unused, pullback = jax.vjp(smooth_act, upper)
-    return pullback(grad_act)[0]
-
-
-def layer_norm(hidden, gain, bias):
-    centre = jnp.mean(hidden, axis=-1, keepdims=True)
-    centered = hidden - centre
-    variance = jnp.mean(centered * centered, axis=-1, keepdims=True)
-    scaled = centered * lax.rsqrt(variance + EPS_NORM)
-    return (scaled, scaled * gain + bias)
+def mm_nn(a, b):
+    return lax.dot_general(a, b, (((1,), (0,)), ((), ())), preferred_element_type=F32)
+
+
+def mm_nt(a, b):
+    return lax.dot_general(a, b, (((1,), (1,)), ((), ())), preferred_element_type=F32)
+
+
+def mm_tn(a, b):
+    return lax.dot_general(a, b, (((0,), (0,)), ((), ())), preferred_element_type=F32)
+
+
+def normalise(v):
+    centered = v - jnp.mean(v, axis=-1, keepdims=True)
+    inverse = lax.rsqrt(jnp.mean(centered * centered, axis=-1, keepdims=True) + EPS_NORM)
+    return centered * inverse, inverse
+
+
+def rows_of(index, size):
+    return pl.ds(pl.multiple_of(index * size, size), size)
+
+
+class Place:
+    def __init__(self, zn, xn, yn):
+        self.zn, self.xn, self.yn = zn, xn, yn
+        self.dp = lax.axis_index("dp")
+        self.seq = lax.axis_index("seq")
+        self.z, self.x = self.dp // xn, lax.rem(self.dp, xn)
+        self.y, self.c = self.seq // CORES, lax.rem(self.seq, CORES)
+
+    def zo(self, k):
+        return lax.rem(self.z + k + self.zn, self.zn)
+
+    def xo(self, k):
+        return lax.rem(self.x + k + self.xn, self.xn)
+
+    def yo(self, k):
+        return lax.rem(self.y + k + self.yn, self.yn)
+
+    def dev(self, dz=0, dx=0, dy=0, dc=0):
+        core = (1 - self.c) if dc else self.c
+        return (self.zo(dz) * self.xn + self.xo(dx), self.yo(dy) * CORES + core)
+
+    def dp_at(self, dz, dx):
+        return self.zo(dz) * self.xn + self.xo(dx)
+
+    def seq_at(self, dy, dc):
+        core = (1 - self.c) if dc else self.c
+        return self.yo(dy) * CORES + core
+
+    def peers(self):
+        out = [self.dev(dc=1)]
+        out += [self.dev(dy=k) for k in range(1, self.yn)]
+        out += [self.dev(dx=k) for k in range(1, self.xn)]
+        out += [self.dev(dz=k) for k in range(1, self.zn)]
+        return out
+
+    def barrier(self):
+        sem = pltpu.get_barrier_semaphore()
+        peers = self.peers()
+        for peer in peers:
+            pl.semaphore_signal(sem, inc=1, device_id=peer, device_id_type=MESH)
+        pl.semaphore_wait(sem, len(peers))
+
+
+def near_first(count):
+    order = []
+    for k in range(1, count):
+        order.append((min(k, count - k), k))
+    return [k for unused, k in sorted(order)]
+
+
+def remote(src, dst, send, recv, dev):
+    return pltpu.make_async_remote_copy(
+        src_ref=src, dst_ref=dst, send_sem=send, recv_sem=recv, device_id=dev, device_id_type=MESH
+    )
+
+
+def all_sum(place, value, slots, send, recv):
+    stages = (
+        (CORES, place.c, lambda k: place.dev(dc=1), lambda k: 1 - place.c),
+        (place.yn, place.y, lambda k: place.dev(dy=k), lambda k: place.yo(-k)),
+        (place.xn, place.x, lambda k: place.dev(dx=k), lambda k: place.xo(-k)),
+        (place.zn, place.z, lambda k: place.dev(dz=k), lambda k: place.zo(-k)),
+    )
+    base = 0
+    at = 0
+    for size, mine, target, origin in stages:
+        slots[base + mine] = value
+        own = slots.at[base + mine]
+        for k in range(1, size):
+            remote(own, own, send.at[at + k - 1], recv.at[at + k - 1], target(k)).start()
+        for k in range(1, size):
+            came = slots.at[base + origin(k)]
+            remote(came, came, send.at[at + k - 1], recv.at[at + k - 1], target(k)).wait_recv()
+        for k in range(1, size):
+            remote(own, own, send.at[at + k - 1], recv.at[at + k - 1], target(k)).wait_send()
+        value = slots[base]
+        for k in range(1, size):
+            value = value + slots[base + k]
+        base += size
+        at += size - 1
+    return value
+
+
+def sum_slots(zn, xn, yn):
+    return CORES + yn + xn + zn, 1 + (yn - 1) + (xn - 1) + (zn - 1)
+
+
+class Gather:
+    def __init__(self, place, buf, block, send, recv):
+        self.p, self.buf, self.block, self.send, self.recv = place, buf, block, send, recv
+
+    def at(self, dy, dc):
+        return self.buf.at[rows_of(self.p.seq_at(dy, dc), self.block)]
+
+    def start(self):
+        p, own = self.p, self.at(0, 0)
+        for k in range(1, p.yn):
+            remote(own, own, self.send.at[k], self.recv.at[k], p.dev(dy=k)).start()
+        remote(own, own, self.send.at[0], self.recv.at[0], p.dev(dc=1)).start()
+
+    def wait_chip(self):
+        came = self.at(0, 1)
+        remote(came, came, self.send.at[0], self.recv.at[0], self.p.dev(dc=1)).wait_recv()
+
+    def forward(self):
+        p = self.p
+        for k in range(1, p.yn):
+            came = self.at(-k, 0)
+            remote(came, came, self.send.at[k], self.recv.at[k], p.dev(dy=k)).wait_recv()
+            f = p.yn - 1 + k
+            remote(came, came, self.send.at[f], self.recv.at[f], p.dev(dc=1)).start()
+
+    def wait_rest(self):
+        p = self.p
+        for k in range(1, p.yn):
+            f = p.yn - 1 + k
+            came = self.at(-k, 1)
+            remote(came, came, self.send.at[f], self.recv.at[f], p.dev(dc=1)).wait_recv()
+        own = self.at(0, 0)
+        for k in range(1, p.yn):
+            remote(own, own, self.send.at[k], self.recv.at[k], p.dev(dy=k)).wait_send()
+            f = p.yn - 1 + k
+            sent = self.at(-k, 0)
+            remote(sent, sent, self.send.at[f], self.recv.at[f], p.dev(dc=1)).wait_send()
+        remote(own, own, self.send.at[0], self.recv.at[0], p.dev(dc=1)).wait_send()
+
+
+class Scatter:
+    def __init__(self, place, sbuf, rbuf, ysend, yrecv, acc, send, recv):
+        self.p = place
+        self.sbuf, self.rbuf, self.ysend, self.yrecv, self.acc = sbuf, rbuf, ysend, yrecv, acc
+        self.send, self.recv = send, recv
+
+    def core(self, k):
+        return remote(
+            self.sbuf.at[k], self.rbuf.at[k], self.send.at[k], self.recv.at[k], self.p.dev(dc=1)
+        )
+
+    def cross(self, k):
+        s = self.p.yn + k - 1
+        return remote(
+            self.ysend.at[k - 1],
+            self.yrecv.at[k - 1],
+            self.send.at[s],
+            self.recv.at[s],
+            self.p.dev(dy=k),
+        )
+
+    def start(self, part):
+        p = self.p
+        for k in list(range(1, p.yn)) + [0]:
+            self.sbuf[k] = part(p.seq_at(k, 1)).astype(BF16)
+            self.core(k).start()
+            mine = part(p.seq_at(k, 0))
+            self.core(k).wait_recv()
+            mine = mine + self.rbuf[k].astype(F32)
+            if k:
+                self.ysend[k - 1] = mine.astype(BF16)
+                self.cross(k).start()
+            else:
+                self.acc[...] = mine
+
+    def wait(self):
+        p = self.p
+        for k in range(1, p.yn):
+            self.cross(k).wait_recv()
+        for k in range(1, p.yn):
+            self.cross(k).wait_send()
+        for k in range(p.yn):
+            self.core(k).wait_send()
+
+    def rows(self, at):
+        value = self.acc[at, :]
+        for k in range(1, self.p.yn):
+            value = value + self.yrecv[k - 1, at, :].astype(F32)
+        return value
+
+
+def row_loop(total, step, fn):
+    def one(i, unused):
+        fn(rows_of(i, step))
+        return unused
+
+    lax.fori_loop(0, total // step, one, 0)
+
+
+def forward_kernel(dims, *refs):
+    (layers, slots, width, block, local_width, local_ff, groups, zn, xn, yn) = dims
+    heads = local_width // HD
+    shard = width // groups
+    refs = list(refs)
+
+    def take(count):
+        out = refs[:count]
+        del refs[:count]
+        return out
+
+    lengths, slopes, x_in, norm_in = take(4)
+    ws = take(4)
+    out, norm_out = take(2)
+    w_save = take(4)
+    xn1_save, xn2_save, qkv_save, ctx_save, lse_save, act_save, dact_save, hid_save, mid_save = take(9)
+    w = take(4)
+    xn1, xn2, qkv, ctx, lse, act, dact, hid, mid, upper = take(10)
+    sbuf, rbuf, ysend, yrecv, acc, nslots = take(6)
+    zsend, zrecv, xsend, xrecv, own_sem, wsave_sem = take(6)
+    ag_send, ag_recv, rs_send, rs_recv, ns_send, ns_recv, save_sem = take(7)
+
+    p = Place(zn, xn, yn)
+    z_order = near_first(zn)
+    length = lengths[0]
+
+    def shard_rows(index):
+        return rows_of(index, shard)
+
+    def z_copy(l, k, dz):
+        at = shard_rows(p.dp)
+        return remote(
+            ws[k].at[l], w[k].at[l, at], zsend.at[l, k, dz - 1], zrecv.at[l, k, dz - 1], p.dev(dz=dz)
+        )
+
+    def z_came(l, k, dz):
+        at = shard_rows(p.dp_at(-dz, 0))
+        return remote(
+            ws[k].at[l], w[k].at[l, at], zsend.at[l, k, dz - 1], zrecv.at[l, k, dz - 1], p.dev(dz=dz)
+        )
+
+    def x_copy(l, k, dx, dz):
+        at = shard_rows(p.dp_at(-dz, 0))
+        src = w[k].at[l, at] if dz else ws[k].at[l]
+        return remote(
+            src, w[k].at[l, at], xsend.at[l, k, dx - 1, dz], xrecv.at[l, k, dx - 1, dz], p.dev(dx=dx)
+        )
+
+    def x_came(l, k, dx, dz):
+        at = shard_rows(p.dp_at(-dz, -dx))
+        return remote(
+            ws[k].at[l],
+            w[k].at[l, at],
+            xsend.at[l, k, dx - 1, dz],
+            xrecv.at[l, k, dx - 1, dz],
+            p.dev(dx=dx),
+        )
+
+    def own_copy(l, k):
+        return pltpu.make_async_copy(ws[k].at[l], w[k].at[l, shard_rows(p.dp)], own_sem.at[l, k])
+
+    def start_own(l, k):
+        for dz in z_order:
+            z_copy(l, k, dz).start()
+        for dx in range(1, xn):
+            x_copy(l, k, dx, 0).start()
+        own_copy(l, k).start()
+
+    def pump(l, k):
+        for dz in z_order:
+            z_came(l, k, dz).wait_recv()
+            for dx in range(1, xn):
+                x_copy(l, k, dx, dz).start()
+
+    def save_weight(l, k):
+        return pltpu.make_async_copy(w[k].at[l], w_save[k].at[l], wsave_sem.at[l, k])
+
+    def need(l, k):
+        own_copy(l, k).wait()
+        for dz in [0] + z_order:
+            for dx in range(1, xn):
+                x_came(l, k, dx, dz).wait_recv()
+        save_weight(l, k).start()
+
+    def finish_weight(l, k):
+        for dz in z_order:
+            z_copy(l, k, dz).wait_send()
+        for dz in range(zn):
+            for dx in range(1, xn):
+                x_copy(l, k, dx, dz).wait_send()
+        save_weight(l, k).wait()
+
+    def save(l, which, src, dst):
+        return pltpu.make_async_copy(src, dst, save_sem.at[l, which])
+
+    def saves(l):
+        return (
+            save(l, 0, xn1.at[l], xn1_save.at[l]),
+            save(l, 1, xn2.at[l], xn2_save.at[l]),
+            save(l, 2, qkv.at[l], qkv_save.at[l]),
+            save(l, 3, ctx.at[l], ctx_save.at[l]),
+            save(l, 4, lse.at[l], lse_save.at[l]),
+            save(l, 5, act.at[l], act_save.at[l]),
+            save(l, 6, dact.at[l], dact_save.at[l]),
+            save(l, 7, hid.at[l], hid_save.at[l]),
+            save(l, 8, mid.at[l], mid_save.at[l]),
+        )
+
+    p.barrier()
+    start_own(0, 0)
+    start_own(0, 1)
+    norm_out[...] = all_sum(p, norm_in[...], nslots, ns_send, ns_recv)
+
+    def load_in(at):
+        hid[0, at, :] = x_in[at, :].astype(F32)
+
+    row_loop(block, 64, load_in)
+    first = p.seq * block
+
+    def norm_row(index):
+        return norm_out[pl.ds(index, 1), :]
+
+    def norm_into(l, source, target, row):
+        gain, bias = norm_row(4 * l + row), norm_row(4 * l + row + 1)
+
+        def one(i, unused):
+            scaled, inverse = normalise(source[l, rows_of(i, 32), :])
+            at = pl.ds(pl.multiple_of(first + i * 32, 32), 32)
+            target[l, at, :] = (scaled * gain + bias).astype(BF16)
+            return unused
+
+        lax.fori_loop(0, block // 32, one, 0)
+
+    def attention(l):
+        key_at = lax.broadcasted_iota(jnp.int32, (1, slots), 1)
+        step = 256
+        causal = lax.broadcasted_iota(jnp.int32, (step, step), 1) <= lax.broadcasted_iota(
+            jnp.int32, (step, step), 0
+        )
+        for h in range(heads):
+            bias = jnp.where(key_at < length, slopes[h] * key_at.astype(F32), -jnp.inf)
+            cols = pl.ds(h * HD, HD)
+            for b in range(slots // step):
+                here = pl.ds(b * step, step)
+                before = pl.ds(0, b * step)
+                k_cols = pl.ds(local_width + h * HD, HD)
+                v_cols = pl.ds(2 * local_width + h * HD, HD)
+                q = qkv[l, here, cols]
+                raw = mm_nt(q, qkv[l, here, k_cols]) * SCORE_SCALE + bias[:, b * step : (b + 1) * step]
+                raw = jnp.where(causal, raw, -jnp.inf)
+                top = jnp.max(raw, axis=1, keepdims=True)
+                if b:
+                    past = mm_nt(q, qkv[l, before, k_cols]) * SCORE_SCALE + bias[:, : b * step]
+                    top = jnp.maximum(top, jnp.max(past, axis=1, keepdims=True))
+                e_here = jnp.exp(raw - top)
+                total = jnp.sum(e_here, axis=1, keepdims=True)
+                value = mm_nn(e_here.astype(BF16), qkv[l, here, v_cols])
+                if b:
+                    e_past = jnp.exp(past - top)
+                    total = total + jnp.sum(e_past, axis=1, keepdims=True)
+                    value = value + mm_nn(e_past.astype(BF16), qkv[l, before, v_cols])
+                ctx[l, here, cols] = (value / total).astype(BF16)
+                lse[l, here, pl.ds(h, 1)] = top + jnp.log(total)
+
+    def layer(l, unused):
+        last = layers - 1
+        g_one = Gather(p, xn1.at[l], block, ag_send.at[2 * l], ag_recv.at[2 * l])
+        g_two = Gather(p, xn2.at[l], block, ag_send.at[2 * l + 1], ag_recv.at[2 * l + 1])
+        rs = [
+            Scatter(
+                p, sbuf, rbuf, ysend, yrecv, acc,
+                rs_send.at[2 * l + i], rs_recv.at[2 * l + i],
+            )
+            for i in range(2)
+        ]
+        save_at = saves(l)
+        save_at[7].start()
+        norm_into(l, hid, xn1, 0)
+        g_one.start()
+
+        @pl.when(l == 0)
+        def _():
+            pump(0, 0)
+            start_own(0, 2)
+
+        def project(index):
+            at = rows_of(index, block)
+            qkv[l, at, :] = mm_nn(xn1[l, at, :], w[0][l]).astype(BF16)
+
+        g_one.wait_chip()
+        g_one.forward()
+        need(l, 0)
+        project(p.seq_at(0, 0))
+        project(p.seq_at(0, 1))
+        g_one.wait_rest()
+        save_at[0].start()
+        for k in range(1, yn):
+            project(p.seq_at(-k, 0))
+            project(p.seq_at(-k, 1))
+        save_at[2].start()
+        attention(l)
+        save_at[3].start()
+        save_at[4].start()
+        pump(l, 1)
+        start_own(l, 3)
+        need(l, 1)
+        rs[0].start(lambda b: mm_nt(ctx[l, rows_of(b, block), :], w[1][l]))
+        pump(l, 2)
+
+        @pl.when(l < last)
+        def _():
+            start_own(l + 1, 0)
+
+        rs[0].wait()
+
+        def add_middle(at):
+            mid[l, at, :] = hid[l, at, :] + rs[0].rows(at)
+
+        row_loop(block, 32, add_middle)
+        save_at[8].start()
+        norm_into(l, mid, xn2, 2)
+        g_two.start()
+        need(l, 2)
+
+        def expand(index):
+            base = pl.multiple_of(index * block, block)
+            upper[...] = mm_nn(xn2[l, pl.ds(base, block), :], w[2][l])
+
+            def one(i, unused):
+                u = upper[rows_of(i, 16), :]
+                at = pl.ds(pl.multiple_of(base + i * 16, 16), 16)
+                square = u * u
+                t = jnp.tanh(GELU_A * u * (1.0 + GELU_B * square))
+                half = 0.5 * (1.0 + t)
+                act[l, at, :] = (u * half).astype(BF16)
+                slope = (0.5 * GELU_A) * u * (1.0 - t * t) * (1.0 + (3.0 * GELU_B) * square)
+                dact[l, at, :] = (half + slope).astype(BF16)
+                return unused
+
+            lax.fori_loop(0, block // 16, one, 0)
+
+        expand(p.seq_at(0, 0))
+        g_two.wait_chip()
+        expand(p.seq_at(0, 1))
+        g_two.forward()
+        pump(l, 3)
+
+        @pl.when(l < last)
+        def _():
+            start_own(l + 1, 1)
+
+        g_two.wait_rest()
+        save_at[1].start()
+        for k in range(1, yn):
+            expand(p.seq_at(-k, 0))
+            expand(p.seq_at(-k, 1))
+        save_at[5].start()
+        save_at[6].start()
+        need(l, 3)
+        rs[1].start(lambda b: mm_nt(act[l, rows_of(b, block), :], w[3][l]))
+
+        @pl.when(l < last)
+        def _():
+            pump(l + 1, 0)
+            start_own(l + 1, 2)
+
+        rs[1].wait()
+
+        @pl.when(l < last)
+        def _():
+            def add_next(at):
+                hid[l + 1, at, :] = mid[l, at, :] + rs[1].rows(at)
+
+            row_loop(block, 32, add_next)
+
+        @pl.when(l == last)
+        def _():
+            def add_out(at):
+                out[at, :] = mid[l, at, :] + rs[1].rows(at)
+
+            row_loop(block, 32, add_out)
+
+        return unused
+
+    lax.fori_loop(0, layers, layer, 0)
+
+    def finish(l, unused):
+        for k in range(4):
+            finish_weight(l, k)
+        for item in saves(l):
+            item.wait()
+        return unused
+
+    lax.fori_loop(0, layers, finish, 0)
+
+
+def run_forward(dims, lengths, slopes, x_in, norm_in, shards):
+    (layers, slots, width, block, local_width, local_ff, groups, zn, xn, yn) = dims
+    cols = (3 * local_width, local_width, local_ff, local_ff)
+    slot_count, sem_count = sum_slots(zn, xn, yn)
+
+    def saved(*shape, dtype=BF16):
+        return jax.ShapeDtypeStruct((layers,) + shape, dtype)
+
+    vmem = pl.BlockSpec(memory_space=pltpu.VMEM)
+    smem = pl.BlockSpec(memory_space=pltpu.SMEM)
+    hbm = pl.BlockSpec(memory_space=pl.ANY)
+    kept = [saved(width, c) for c in cols] + [
+        saved(slots, width),
+        saved(slots, width),
+        saved(slots, 3 * local_width),
+        saved(slots, local_width),
+        saved(slots, 128, dtype=F32),
+        saved(slots, local_ff),
+        saved(slots, local_ff),
+        saved(block, width, dtype=F32),
+        saved(block, width, dtype=F32),
+    ]
+    dma = pltpu.SemaphoreType.DMA
+    return pl.pallas_call(
+        functools.partial(forward_kernel, dims),
+        out_shape=[
+            jax.ShapeDtypeStruct((block, width), F32),
+            jax.ShapeDtypeStruct((4 * layers, width), F32),
+        ]
+        + kept,
+        in_specs=[smem, smem] + [vmem] * 6,
+        out_specs=[vmem, vmem] + [hbm] * len(kept),
+        scratch_shapes=[pltpu.VMEM(k.shape, k.dtype) for k in kept]
+        + [
+            pltpu.VMEM((block, local_ff), F32),
+            pltpu.VMEM((yn, block, width), BF16),
+            pltpu.VMEM((yn, block, width), BF16),
+            pltpu.VMEM((yn - 1, block, width), BF16),
+            pltpu.VMEM((yn - 1, block, width), BF16),
+            pltpu.VMEM((block, width), F32),
+            pltpu.VMEM((slot_count, 4 * layers, width), F32),
+            dma((layers, 4, zn - 1)),
+            dma((layers, 4, zn - 1)),
+            dma((layers, 4, xn - 1, zn)),
+            dma((layers, 4, xn - 1, zn)),
+            dma((layers, 4)),
+            dma((layers, 4)),
+            dma((2 * layers, 2 * yn - 1)),
+            dma((2 * layers, 2 * yn - 1)),
+            dma((2 * layers, 2 * yn - 1)),
+            dma((2 * layers, 2 * yn - 1)),
+            dma((sem_count,)),
+            dma((sem_count,)),
+            dma((layers, 9)),
+        ],
+        compiler_params=pltpu.CompilerParams(
+            collective_id=0, has_side_effects=True, vmem_limit_bytes=60 * 2**20
+        ),
+        name="forward_layers",
+    )(lengths, slopes, x_in, norm_in, *shards)
 
 
 def norm_back(hidden, gain, grad_out):
@@ -53,21 +614,6 @@
     return (grad_hidden, jnp.sum(grad_out * scaled, axis=0), jnp.sum(grad_out, axis=0))
 
 
-def pack_layer(masters, layer_index):
-    qkv, proj, up, down = (masters[i][layer_index].astype(jnp.bfloat16) for i in range(4))
-    return qkv.reshape(qkv.shape[0], -1), proj, up, down
-
-
-def gather_layer(masters, layer_index):
-    qkv, proj, up, down = pack_layer(masters, layer_index)
-    return (
-        lax.all_gather(qkv, "dp", axis=0, tiled=True),
-        lax.all_gather(proj, "dp", axis=1, tiled=True),
-        lax.all_gather(up, "dp", axis=0, tiled=True),
-        lax.all_gather(down, "dp", axis=1, tiled=True),
-    )
-
-
 def scatter_sum(part, axis_name, dimension):
     return lax.psum_scatter(
         part.astype(jnp.bfloat16), axis_name, scatter_dimension=dimension, tiled=True
@@ -82,37 +628,12 @@
     ) * HD ** (-0.5)
     query_pos = first_row + jnp.arange(block_rows, dtype=jnp.int32)
     key_pos = jnp.arange(slot_count, dtype=jnp.int32)
-    distance = (key_pos[None, :] - query_pos[:, None]).astype(jnp.float32)
+    distance = jnp.broadcast_to(key_pos[None, :], (block_rows, slot_count)).astype(jnp.float32)
     raw = raw + slopes[None, :, None, None] * distance[None, None]
     causal = key_pos[None, :] <= query_pos[:, None]
     filled = key_pos[None, :] < lengths[:, None]
     allowed = causal[None, None] & filled[:, None, None, :]
     return jnp.where(allowed, raw, -jnp.inf)
-
-
-def attend_forward(queries, key_rows, values, slopes, lengths):
-    row_count, slot_count, head_local, head_size = queries.shape
-    block_rows = min(512, slot_count)
-
-    def one_block(block_index, carry):
-        context, log_total = carry
-        first_row = block_index * block_rows
-        query_block = lax.dynamic_slice_in_dim(queries, first_row, block_rows, 1)
-        scores = block_scores(query_block, key_rows, first_row, slopes, lengths)
-        block_total = jax.nn.logsumexp(scores, axis=3, keepdims=True)
-        attention = jnp.exp(scores - block_total).astype(jnp.bfloat16)
-        block_context = jnp.einsum(
-            "rhqk,rkhd->rqhd", attention, values, preferred_element_type=jnp.float32
-        ).astype(jnp.bfloat16)
-        context = lax.dynamic_update_slice_in_dim(context, block_context, first_row, 1)
-        log_total = lax.dynamic_update_slice_in_dim(log_total, block_total[..., 0], first_row, 2)
-        return (context, log_total)
-
-    initial = (
-        jnp.zeros(queries.shape, jnp.bfloat16),
-        jnp.zeros((row_count, head_local, slot_count), jnp.float32),
-    )
-    return lax.fori_loop(0, slot_count // block_rows, one_block, initial)
 
 
 def attend_backward(queries, key_rows, values, grad_context, log_total, slopes, lengths):
@@ -190,74 +711,56 @@
     down_second,
     norm_second,
 ):
-    masters = (qkv_weight, proj_weight, up_weight, down_weight, norm_params)
-    row_count, local_slots, model_width = block_input.shape
+    row_count, local_slots, width = block_input.shape
     seq_count = lax.axis_size("seq")
-    head_local = H // seq_count
-    token_count = row_count * local_slots
+    groups = lax.axis_size("dp")
     layer_count = qkv_weight.shape[0]
-    table = jnp.asarray(slope_table(H), jnp.float32)
+    slots = local_slots * seq_count
+    local_width = qkv_weight.shape[3]
+    local_ff = up_weight.shape[2]
+    head_local = local_width // HD
+    dims = (
+        layer_count, slots, width, local_slots, local_width, local_ff, groups,
+        ZSIZE, groups // ZSIZE, seq_count // CORES,
+    )
     head_ids = lax.axis_index("seq") * head_local + jnp.arange(head_local, dtype=jnp.int32)
-    slopes = jnp.sum(
-        jnp.where(
-            jnp.arange(H, dtype=jnp.int32)[None, :] == head_ids[:, None], table[None, :], 0.0
-        ),
-        axis=1,
-    )
-    hidden = block_input.astype(jnp.float32).reshape(token_count, model_width)
-    local_width = head_local * HD
-    group_count = lax.axis_size("dp")
-    norm_piece = norm_params.shape[2]
-    norm_all = lax.all_gather(
-        norm_params.astype(jnp.bfloat16), ("dp", "seq"), axis=2, tiled=True
-    ).astype(jnp.float32)
-    saved = []
-    for layer_index in range(layer_count):
-        w_qkv, w_proj, w_up, w_down = gather_layer(masters, layer_index)
-        norm_rows = norm_all[layer_index]
-        unused, normed = layer_norm(hidden, norm_rows[0], norm_rows[1])
-        normed_one = lax.all_gather(normed.astype(jnp.bfloat16), "seq", axis=0, tiled=True)
-        projected = jnp.dot(normed_one, w_qkv, preferred_element_type=jnp.float32).astype(
-            jnp.bfloat16
-        )
-        spread = projected.reshape(row_count, local_slots * seq_count, 3, head_local, HD)
-        context, log_total = attend_forward(
-            spread[:, :, 0], spread[:, :, 1], spread[:, :, 2], slopes, row_lengths
-        )
-        context_rows = context.reshape(-1, local_width)
-        middle = hidden + scatter_sum(
-            jnp.dot(context_rows, w_proj, preferred_element_type=jnp.float32), "seq", 0
-        )
-        unused, normed_two = layer_norm(middle, norm_rows[2], norm_rows[3])
-        normed_two = lax.all_gather(normed_two.astype(jnp.bfloat16), "seq", axis=0, tiled=True)
-        upper = jnp.dot(normed_two, w_up, preferred_element_type=jnp.float32)
-        act_low = smooth_act(upper).astype(jnp.bfloat16)
-        following = middle + scatter_sum(
-            jnp.dot(act_low, w_down, preferred_element_type=jnp.float32), "seq", 0
-        )
-        saved.append(
-            (hidden, middle, spread, log_total, context_rows, act_low, upper, normed_one,
-             normed_two, (w_qkv, w_proj, w_up, w_down, norm_rows))
-        )
-        hidden = following
-    block_output = hidden.reshape(row_count, local_slots, model_width)
+    slopes = jnp.asarray(slope_table(H), F32)[head_ids]
+    shards = (
+        qkv_weight.astype(BF16).reshape(layer_count, -1, 3 * local_width),
+        jnp.swapaxes(proj_weight.astype(BF16), 1, 2),
+        up_weight.astype(BF16),
+        jnp.swapaxes(down_weight.astype(BF16), 1, 2),
+    )
+    piece = norm_params.shape[2]
+    device_at = lax.axis_index("dp") * seq_count + lax.axis_index("seq")
+    norm_local = norm_params.astype(BF16).astype(F32).reshape(4 * layer_count, piece)
+    norm_in = lax.dynamic_update_slice(
+        jnp.zeros((4 * layer_count, width), F32), norm_local, (0, device_at * piece)
+    )
+    kept = run_forward(
+        dims, row_lengths, slopes, block_input.reshape(local_slots, width), norm_in, shards
+    )
+    block_output = kept[0].reshape(row_count, local_slots, width)
+    norm_all = kept[1].reshape(layer_count, 4, width)
     positions = lax.axis_index("seq") * local_slots + jnp.arange(local_slots, dtype=jnp.int32)
     token_mask = (positions[None, :] < row_lengths[:, None]).astype(jnp.float32)
     grad_hidden = (output_grad.astype(jnp.float32) * token_mask[:, :, None]).reshape(
-        token_count, model_width
+        local_slots * row_count, width
     )
     reduced_all = [None] * layer_count
     norm_parts = [None] * layer_count
     for layer_index in reversed(range(layer_count)):
-        (hidden_in, middle, spread, log_total, context_rows, act_low, upper, normed_one,
-         normed_two, weights) = saved[layer_index]
-        w_qkv, w_proj, w_up, w_down, norm_rows = weights
+        (w_qkv, w_proj_t, w_up, w_down_t, normed_one, normed_two, qkv_rows, context_rows, log_all,
+         act_low, act_slope, hidden_in, middle) = (item[layer_index] for item in kept[2:])
+        norm_rows = norm_all[layer_index]
+        spread = qkv_rows.reshape(row_count, slots, 3, head_local, HD)
+        log_total = log_all[:, :head_local].T[None]
         grad_ffn = lax.all_gather(grad_hidden.astype(jnp.bfloat16), "seq", axis=0, tiled=True)
         down_grad = scatter_sum(
             jnp.einsum("tf,td->fd", act_low, grad_ffn, preferred_element_type=jnp.float32), "dp", 1
         )
-        grad_act = jnp.einsum("td,fd->tf", grad_ffn, w_down, preferred_element_type=jnp.float32)
-        grad_upper = smooth_back(upper, grad_act).astype(jnp.bfloat16)
+        grad_act = jnp.einsum("td,df->tf", grad_ffn, w_down_t, preferred_element_type=jnp.float32)
+        grad_upper = (grad_act * act_slope.astype(F32)).astype(jnp.bfloat16)
         up_grad = scatter_sum(
             jnp.einsum("td,tf->df", normed_two, grad_upper, preferred_element_type=jnp.float32),
             "dp", 0,
@@ -273,7 +776,7 @@
             "dp", 1,
         )
         grad_context = jnp.einsum(
-            "te,de->td", grad_branch, w_proj, preferred_element_type=jnp.float32
+            "te,ed->td", grad_branch, w_proj_t, preferred_element_type=jnp.float32
         ).astype(jnp.bfloat16)
         grad_context = grad_context.reshape(row_count, -1, head_local, HD)
         grad_queries, grad_keys, grad_values = attend_backward(
@@ -295,7 +798,7 @@
         grad_hidden = grad_middle + grad_input_norm
         norm_parts[layer_index] = jnp.stack((gain_one, bias_one, gain_two, bias_two), axis=0)
         reduced_all[layer_index] = (qkv_grad, proj_grad, up_grad, down_grad)
-    input_grad = grad_hidden.reshape(row_count, local_slots, model_width)
+    input_grad = grad_hidden.reshape(row_count, local_slots, width)
     norm_grad = lax.psum_scatter(
         jnp.stack(norm_parts, axis=0), ("dp", "seq"), scatter_dimension=2, tiled=True
     )

time: 1690 us -> 1270 us (0.75)
  waiting for transfers between devices: 1180 us -> 757 us
  Pallas kernels: 0 us -> 221 us
  blocking collectives: 142 us -> 36.8 us
  matrix products: 155 us -> 82.4 us
  other arithmetic: 78.4 us -> 48.8 us
    all_gather x10 -> x0, waiting for transfers between devices: 280 us -> none  [the longest x2 101 us: gather_layer(): lax.all_gather(down, 'dp', axis=1, tiled=True)]
    pallas_call x0 -> x1, Pallas kernels: none -> 221 us  [run_forward(): pl.pallas_call(functools.partial(forward_kernel, dims), out_shape=[jax.Sh...]
    reduce_scatter x12 -> x8, waiting for transfers between devices: 499 us -> 387 us  [scatter_sum(): lax.psum_scatter(part.astype(jnp.bfloat16), axis_name, scatter_dimension=...]
    all_gather x3 -> x0, blocking collectives: 105 us -> none  [the longest x2 59.6 us: gather_layer(): lax.all_gather(proj, 'dp', axis=1, tiled=True)]
    dot_general x16 -> x4, matrix products: 69.9 us -> 15.5 us  [the longest x2 10.7 us: body(): jnp.einsum('td,df->tf', grad_ffn, w_down_t, preferred_element_type=jnp.fl...]
    slice x5 -> x2, local copies, waits for them, and re-layouts: 29.8 us -> 4.4 us  [the longest x1 3.8 us: body(): item[layer_index]]
    all_gather x2, waiting for transfers between devices: 40.6 us -> 22.7 us  [body(): lax.all_gather(grad_hidden.astype(jnp.bfloat16), 'seq', axis=0, tiled=True)]
    unnamed x152 -> x135, local copies, waits for them, and re-layouts: 38.4 us -> 44.2 us
  transfers between devices with their start and end apart: 31 -> 17, of which waited for: 28 -> 15; matrix products, arithmetic and copies ran while one was open for 10% -> 9% of each run, Pallas kernels for 0% -> 18%
where the time goes in v2:
time: 1270 us; the launch traced here: 1250 us
  waiting for transfers between devices  757 us (60%)
  Pallas kernels  221 us (17%)
  matrix products  82.4 us (6%)
  local copies, waits for them, and re-layouts  81 us (6%)
  other arithmetic  48.8 us (4%)
  blocking collectives  36.8 us (3%)
  between operations  20.8 us (2%)
    reduce_scatter x8, waiting for transfers between devices, scatter_sum(): lax.psum_scatter(part.astype(jnp.bfloat16), axis_name, scatter_dimension=...  387 us
    unnamed x22, waiting for transfers between devices  339 us
    pallas_call x1, Pallas kernels, run_forward(): pl.pallas_call(functools.partial(forward_kernel, dims), out_shape=[jax.Sh...  221 us
    unnamed x135, local copies, waits for them, and re-layouts  44.2 us
    psum x1, blocking collectives, body(): grad_norm = jnp.sqrt(lax.psum(square_sum, ('dp', 'seq')))  36.8 us
  transfers between devices with their start and end apart: 17, of which 15 were waited for; matrix products, arithmetic and copies ran while one was open for 9% of the time, Pallas kernels for 18%

profile of v2, /device:TPU:0, one launch (start us, length us, event | category | flops | bytes accessed | tf_op | source)
XLA Modules:
  0.0 1249.8 jit_solution(12400083991732645945)
XLA Ops:
  17.3 221.3 %forward_layers.1 = (f32[256,1024]{1,0:T(8,128)}, f32[8,1024]{1,0:T(8,128)}, bf16[2,1024,768]{2,1,0:T(8,128)(2,1)}, bf16[2,1024,256]{2,1,0:T(8,128)(2,1)}, bf16[...) custom-call(s32[1]{0:T(128)} %copy.196.refs_0_, ...), custom_call_target="tpu_custom_call" | custom-call | tf_op jit(solution)/shard_map/forward_layers/pallas_call | solution.py:565
  238.6 5.3 fusion.59
  251.7 28.2 %reduce-scatter.24.cloned.1.call-done = bf16[256,1024]{1,0:T(8,128)(2,1)} async-done(((bf16[1024,1024]{1,0:T(8,128)(2,1)}), bf16[256,1024]{1,0:T(8,128)(2,1)}) %reduce-scatter.24.cloned.1.call-update) | async-done | bytes 524304 | tf_op jit(solution)/shard_map/reduce_scatter | solution.py:618
  298.6 8.0 all-gather.7.cloned.1.call-done
  309.9 18.1 %while.36 = (s32[]{:T(128)}, bf16[1,1024,2,128]{1,3,2,0:T(8,128)(2,1)}, f32[1,1024,2,128]{1,3,2,0:T(8,128)S(1)}, f32[1,1024,2,128]{1,3,2,0:T(8,128)S(1)}, s32[1]...) while((s32[]{:T(128)}, ...), condition=%wide.region_9.0_spmd.clone, body=%wide.region_7.9_spmd.clone.sunk | while | flops 1356334592 | bytes 44862240 | solution.py:682
  335.6 29.6 %reduce-scatter.26.cloned.1.call-done = bf16[256,1024]{1,0:T(8,128)(2,1)} async-done(((bf16[1024,1024]{1,0:T(8,128)(2,1)}), bf16[256,1024]{1,0:T(8,128)(2,1)}) %reduce-scatter.26.cloned.1.call-update) | async-done | bytes 524304 | tf_op jit(solution)/shard_map/reduce_scatter | solution.py:618
  368.6 22.7 %all-gather.9.cloned.1.call-done = bf16[1024,1024]{1,0:T(8,128)(2,1)} async-done(((bf16[256,1024]{1,0:T(8,128)(2,1)}), bf16[1024,1024]{1,0:T(8,128)(2,1)}) %all-gather.9.cloned.1.call-update) | async-done | bytes 2097168 | tf_op jit(solution)/shard_map/all_gather | solution.py:758
  391.3 5.3 fusion.58
  401.8 31.5 %reduce-scatter.28.cloned.1.call-done = bf16[256,1024]{1,0:T(8,128)(2,1)} async-done(((bf16[1024,1024]{1,0:T(8,128)(2,1)}), bf16[256,1024]{1,0:T(8,128)(2,1)}) %reduce-scatter.28.cloned.1.call-update) | async-done | bytes 524304 | tf_op jit(solution)/shard_map/reduce_scatter | solution.py:618
  449.5 5.1 fusion.109
  454.9 4.6 fusion.100
  463.7 5.3 fusion.97
  490.1 18.1 %while.37 = (s32[]{:T(128)}, bf16[1,1024,2,128]{1,3,2,0:T(8,128)(2,1)}, f32[1,1024,2,128]{1,3,2,0:T(8,128)S(1)}, f32[1,1024,2,128]{1,3,2,0:T(8,128)S(1)}, s32[1]...) while((s32[]{:T(128)}, ...), condition=%wide.region_22.23_spmd.clone, body=%wide.region_20.0_spmd.clone.sunk | while | flops 1356334592 | bytes 44862240 | solution.py:682
  521.8 10.3 reduce-scatter.46.cloned.1.call-done
  533.2 64.1 %reduce-scatter.42.cloned.1.call-done = bf16[128,256]{1,0:T(8,128)(2,1)} async-done(((bf16[1024,256]{1,0:T(8,128)(2,1)}), bf16[128,256]{1,0:T(8,128)(2,1)}) %reduce-scatter.42.cloned.1.call-update) | async-done | bytes 65552
  598.3 66.2 %reduce-scatter.34.cloned.1.call-done = bf16[128,768]{1,0:T(8,128)(2,1)} async-done(((bf16[1024,768]{1,0:T(8,128)(2,1)}), bf16[128,768]{1,0:T(8,128)(2,1)}) %reduce-scatter.34.cloned.1.call-update) | async-done | bytes 196624 | tf_op jit(solution)/shard_map/reduce_scatter | solution.py:618
  665.6 69.6 %reduce-scatter.44.cloned.1.call-done = bf16[128,1024]{1,0:T(8,128)(2,1)} async-done(((bf16[1024,1024]{1,0:T(8,128)(2,1)}), bf16[128,1024]{1,0:T(8,128)(2,1)}) %reduce-scatter.44.cloned.1.call-update) | async-done | bytes 262160
  736.3 69.3 %reduce-scatter.38.cloned.1.call-done = bf16[128,1024]{1,0:T(8,128)(2,1)} async-done(((bf16[1024,1024]{1,0:T(8,128)(2,1)}), bf16[128,1024]{1,0:T(8,128)(2,1)}) %reduce-scatter.38.cloned.1.call-update) | async-done | bytes 262160 | tf_op jit(solution)/shard_map/reduce_scatter | solution.py:618
  805.6 70.5 %reduce-scatter.36.cloned.1.call-done = bf16[128,1024]{1,0:T(8,128)(2,1)} async-done(((bf16[1024,1024]{1,0:T(8,128)(2,1)}), bf16[128,1024]{1,0:T(8,128)(2,1)}) %reduce-scatter.36.cloned.1.call-update) | async-done | bytes 262160 | tf_op jit(solution)/shard_map/reduce_scatter | solution.py:618
  880.7 60.5 %reduce-scatter.40.cloned.1.call-done = bf16[128,256]{1,0:T(8,128)(2,1)} async-done(((bf16[1024,256]{1,0:T(8,128)(2,1)}), bf16[128,256]{1,0:T(8,128)(2,1)}) %reduce-scatter.40.cloned.1.call-update) | async-done | bytes 65552
  943.5 64.8 %reduce-scatter.32.cloned.1.call-done = bf16[128,768]{1,0:T(8,128)(2,1)} async-done(((bf16[1024,768]{1,0:T(8,128)(2,1)}), bf16[128,768]{1,0:T(8,128)(2,1)}) %reduce-scatter.32.cloned.1.call-update) | async-done | bytes 196624 | tf_op jit(solution)/shard_map/reduce_scatter | solution.py:618
  1014.1 27.2 %reduce-scatter.30.cloned.1.call-done = bf16[256,1024]{1,0:T(8,128)(2,1)} async-done(((bf16[1024,1024]{1,0:T(8,128)(2,1)}), bf16[256,1024]{1,0:T(8,128)(2,1)}) %reduce-scatter.30.cloned.1.call-update) | async-done | bytes 524304 | tf_op jit(solution)/shard_map/reduce_scatter | solution.py:618
  1047.4 133.9 %reduce-scatter.48.cloned.1.call-done = f32[32,8]{1,0:T(8,128)} async-done(((f32[1024,8]{1,0:T(8,128)}), f32[32,8]{1,0:T(8,128)}) %reduce-scatter.48.cloned.1.call-update) | async-done | bytes 1040
  1186.2 36.8 %psum.7 = f32[]{:T(128)} all-reduce(f32[]{:T(128)S(6)} %add.350), channel_id=1, replica_groups=mesh['dp'=8,'seq'=4] {'dp','seq'}, use_global_device_ids=true, to_apply=%region_48.49 | all-reduce | flops 1 | bytes 8 | tf_op jit(solution)/shard_map/psum | solution.py:816
  (328 shorter events, 188.5 us)
Async XLA Ops:
  7.2 231.4 %all-gather.5.cloned.1.call-start = ((), (), s32[]{:S(2)}) async-start(), calls=%async_computation.13 | async-start | bytes 2621440 | tf_op jit(solution)/shard_map/all_gather | solution.py:758
  10.1 269.8 %reduce-scatter.24.cloned.1.call-start = ((), (), s32[]{:S(2)}) async-start(), calls=%async_computation.14 | async-start | bytes 2621440 | tf_op jit(solution)/shard_map/reduce_scatter | solution.py:618
  14.8 223.8 %copy-start.5 = (f32[2,128,3,256]{1,3,2,0:T(8,128)}, f32[2,128,3,256]{1,3,2,0:T(8,128)S(1)}, u32[]{:S(2)}) copy-start(f32[2,128,3,256]{1,3,2,0:T(8,128)S(1)} %copy.103) | copy-start | bytes 2359300
  249.1 57.6 %all-gather.7.cloned.1.call-start = ((), (), s32[]{:S(2)}) async-start(), calls=%async_computation.15 | async-start | bytes 2621440 | tf_op jit(solution)/shard_map/all_gather | solution.py:773
  283.9 81.3 %reduce-scatter.26.cloned.1.call-start = ((), (), s32[]{:S(2)}) async-start(), calls=%async_computation.16 | async-start | bytes 2621440 | tf_op jit(solution)/shard_map/reduce_scatter | solution.py:618
  333.6 57.7 %all-gather.9.cloned.1.call-start = ((), (), s32[]{:S(2)}) async-start(), calls=%async_computation.17 | async-start | bytes 2621440 | tf_op jit(solution)/shard_map/all_gather | solution.py:758
  368.6 64.7 %reduce-scatter.28.cloned.1.call-start = ((), (), s32[]{:S(2)}) async-start(), calls=%async_computation.18 | async-start | bytes 2621440 | tf_op jit(solution)/shard_map/reduce_scatter | solution.py:618
  401.7 81.6 %all-gather.11.cloned.1.call-start = ((), (), s32[]{:S(2)}) async-start(), calls=%async_computation.19 | async-start | bytes 2621440 | tf_op jit(solution)/shard_map/all_gather | solution.py:773
  437.5 94.6 %reduce-scatter.46.cloned.1.call-start = ((), (), s32[]{:S(2)}) async-start(), calls=%async_computation.28 | async-start | bytes 2359296
  444.8 152.5 %reduce-scatter.42.cloned.1.call-start = ((), (), s32[]{:S(2)}) async-start(), calls=%async_computation.26 | async-start | bytes 589824
  449.5 215.0 %reduce-scatter.34.cloned.1.call-start = ((), (), s32[]{:S(2)}) async-start(), calls=%async_computation.22 | async-start | bytes 1769472 | tf_op jit(solution)/shard_map/reduce_scatter | solution.py:618
  454.6 280.6 %reduce-scatter.44.cloned.1.call-start = ((), (), s32[]{:S(2)}) async-start(), calls=%async_computation.27 | async-start | bytes 2359296
  462.1 343.5 %reduce-scatter.38.cloned.1.call-start = ((), (), s32[]{:S(2)}) async-start(), calls=%async_computation.24 | async-start | bytes 2359296 | tf_op jit(solution)/shard_map/reduce_scatter | solution.py:618
  469.0 407.1 %reduce-scatter.36.cloned.1.call-start = ((), (), s32[]{:S(2)}) async-start(), calls=%async_computation.23 | async-start | bytes 2359296 | tf_op jit(solution)/shard_map/reduce_scatter | solution.py:618
  482.8 458.4 %reduce-scatter.40.cloned.1.call-start = ((), (), s32[]{:S(2)}) async-start(), calls=%async_computation.25 | async-start | bytes 589824
  508.3 500.1 %reduce-scatter.32.cloned.1.call-start = ((), (), s32[]{:S(2)}) async-start(), calls=%async_computation.21 | async-start | bytes 1769472 | tf_op jit(solution)/shard_map/reduce_scatter | solution.py:618
  513.8 527.5 %reduce-scatter.30.cloned.1.call-start = ((), (), s32[]{:S(2)}) async-start(), calls=%async_computation.20 | async-start | bytes 2621440 | tf_op jit(solution)/shard_map/reduce_scatter | solution.py:618
  518.4 147.1 %copy-start.40 = (f32[1024]{0:T(1024)S(1)}, f32[1024]{0:T(1024)}, u32[]{:S(2)}) copy-start(f32[1024]{0:T(1024)} %get-tuple-element.636) | copy-start | bytes 12292
  518.4 147.1 %copy-start.41 = (f32[1024]{0:T(1024)S(1)}, f32[1024]{0:T(1024)}, u32[]{:S(2)}) copy-start(f32[1024]{0:T(1024)} %get-tuple-element.651) | copy-start | bytes 12292
  518.4 662.8 %reduce-scatter.48.cloned.1.call-start = ((), (), s32[]{:S(2)}) async-start(), calls=%async_computation.29 | async-start | bytes 540672
  665.6 375.7 %copy-start.43 = (f32[256]{0:T(256)}, f32[256]{0:T(256)S(1)}, u32[]{:S(2)}) copy-start(f32[256]{0:T(256)S(1)} %add_rsqrt_fusion) | copy-start | bytes 3076
  880.7 160.6 %copy-start.2 = (f32[2,256,1024]{2,1,0:T(8,128)S(1)}, f32[2,256,1024]{2,1,0:T(8,128)}, u32[]{:S(2)}) copy-start(f32[2,256,1024]{2,1,0:T(8,128)} %get-tuple-element.421) | copy-start | bytes 6291460
  880.7 160.6 %copy-start.38 = (f32[1,1024]{1,0:T(1,128)S(1)}, f32[1,1024]{1,0:T(1,128)}, u32[]{:S(2)}) copy-start(f32[1,1024]{1,0:T(1,128)} %get-tuple-element.741) | copy-start | bytes 12292
  1047.3 176.4 %copy-start.6 = (f32[2,128,3,256]{1,3,2,0:T(8,128)S(1)}, f32[2,128,3,256]{1,3,2,0:T(8,128)}, u32[]{:S(2)}) copy-start(f32[2,128,3,256]{1,3,2,0:T(8,128)} %copy-done.5) | copy-start | bytes 2359300
  (55 other events, 446.3 us)
Sparse Core Ops, SparseCore 0:
  10.2 25.9 all-gather.4
  249.2 30.6 reduce-scatter.23
  284.0 22.5 all-gather.6
  333.7 31.4 reduce-scatter.25
  368.7 22.5 all-gather.8
  401.8 31.4 reduce-scatter.27
  437.6 22.5 all-gather.10
  464.2 67.8 reduce-scatter.45
  536.4 60.8 reduce-scatter.41
  600.6 63.8 reduce-scatter.33
  668.4 66.7 reduce-scatter.43
  739.0 66.5 reduce-scatter.37
  809.5 66.5 reduce-scatter.35
  880.3 60.9 reduce-scatter.39
  944.5 63.8 reduce-scatter.31
  1010.9 30.3 reduce-scatter.29
  1047.5 133.7 reduce-scatter.47
